TPU v7x, 512 devices: a whole 4x4x16 slice. The times are simulated.
512 devices in a mesh: grid: 128 (over z, y, core), band: 4 (over x).
Axes of the slice: x: 4, y: 4, z: 16, core: 2. Of those that a mesh axis runs over, the one named last changes fastest.
Arguments:
- orbitals: bfloat16 [1024, 131072], P(('grid', 'band')), may hold values from -6 to 128
- pivots: int32 [1024], replicated, may hold values from 0 to 131071, as said below
Outputs:
- localized: bfloat16 [1024, 131072], P(('grid', 'band'))
Inputs may be any that keep to these rules, and one draw needn't show every extreme that they name: Distinct grid points. Pivot j belongs to block (j // 2) % 4; in every block at most 8 pivots lie in one slab of 1024 consecutive grid points, and in every block some slab holds exactly 8 of them.
All inputs are finite; a program needn't handle non-finite values.
Results may differ from a plain program's by a relative error of at most 0.0044.
The roundings to bfloat16 on the way count: a program that leaves them out, or rounds other values in their place, can miss the bound.
Values may be sent and summed in bfloat16 or wider, within the bound.
A program may use at most 128 MiB of HBM per device.

v0:
```python
import math

import jax
import jax.numpy as jnp
from jax import lax
from jax.sharding import PartitionSpec as P


def mixed_index(grid_count, band_count, rows_each):
    total = grid_count * band_count * rows_each
    natural = jnp.arange(total, dtype=jnp.int32)
    inner = natural % rows_each
    block = natural // rows_each % band_count
    outer = natural // (rows_each * band_count)
    return (block * grid_count + outer) * rows_each + inner


def natural_index(grid_count, band_count, rows_each):
    total = grid_count * band_count * rows_each
    mixed = jnp.arange(total, dtype=jnp.int32)
    inner = mixed % rows_each
    outer = mixed // rows_each % grid_count
    block = mixed // (rows_each * grid_count)
    return (outer * band_count + block) * rows_each + inner


def body(orbitals, pivots):
    rows_each = orbitals.shape[0]
    grid_count = lax.axis_size("grid")
    band_count = lax.axis_size("band")
    grid_rank = lax.axis_index("grid")
    band_rank = lax.axis_index("band")
    all_points = orbitals.shape[1]
    slab_width = all_points // grid_count
    bands = rows_each * grid_count * band_count
    block_rows = bands // band_count
    slot_count = min(4 * block_rows // grid_count, block_rows // 4)
    to_mixed = mixed_index(grid_count, band_count, rows_each)
    to_natural = natural_index(grid_count, band_count, rows_each)
    slab_own = lax.all_to_all(orbitals, "grid", split_axis=1, concat_axis=0, tiled=True)
    table = jnp.take(pivots, to_natural, axis=0).reshape(band_count, block_rows)
    owner = table // slab_width
    offset = table % slab_width
    counter = jnp.arange(block_rows, dtype=jnp.int32)
    same_owner = (owner[:, :, None] == owner[:, None, :]) & (
        counter[None, None, :] < counter[None, :, None]
    )
    position = jnp.sum(same_owner.astype(jnp.int32), axis=2)
    picked = (owner == grid_rank)[:, :, None] & (
        position[:, :, None] == jnp.arange(slot_count, dtype=jnp.int32)[None, None, :]
    )
    slot_point = jnp.sum(jnp.where(picked, offset[:, :, None], 0), axis=1)
    filled = jnp.any(picked, axis=1).reshape(band_count * slot_count)
    values = jnp.take(slab_own, slot_point.reshape(band_count * slot_count), axis=1).T
    packed = jnp.where(filled[:, None], values, jnp.zeros((), jnp.bfloat16))
    sorted_slots = lax.all_to_all(packed, "band", split_axis=0, concat_axis=1, tiled=True)
    arrived = lax.all_gather(sorted_slots, "grid", axis=0, tiled=True)
    my_owner = jnp.take(owner, band_rank, axis=0)
    my_position = jnp.take(position, band_rank, axis=0)
    pivot_rows = jnp.take(arrived, my_owner * slot_count + my_position, axis=0)
    scale = 1.0 / math.sqrt(bands)
    contract = (((1,), (1,)), ((), ()))
    slab = lax.all_gather(slab_own, "band", axis=0, tiled=True)
    products = (jnp.dot(pivot_rows, slab, preferred_element_type=jnp.float32) * scale).astype(
        jnp.bfloat16
    )
    gathered = lax.all_gather(products, "band", axis=0, tiled=True)
    local_columns = (
        lax.dot_general(gathered, products, contract, preferred_element_type=jnp.float32)
        / all_points
    )
    gram_columns = lax.psum(local_columns, "grid")
    gram_mixed = lax.all_gather(gram_columns, "band", axis=1, tiled=True)
    gram = jnp.take(jnp.take(gram_mixed, to_mixed, axis=0), to_mixed, axis=1)
    factor = jnp.linalg.cholesky(gram)
    targets = (
        (jnp.arange(grid_count, dtype=jnp.int32)[:, None] * band_count + band_rank) * rows_each
        + jnp.arange(rows_each, dtype=jnp.int32)[None, :]
    ).reshape(block_rows)
    unit_columns = (jnp.arange(bands, dtype=jnp.int32)[:, None] == targets[None, :]).astype(
        jnp.float32
    )
    solved = lax.linalg.triangular_solve(
        factor, unit_columns, left_side=True, lower=True, transpose_a=True
    )
    inverse_rows = solved.T.astype(jnp.bfloat16)
    mixed_rows = jnp.take(inverse_rows, to_natural, axis=1)
    local_result = jnp.dot(mixed_rows, gathered, preferred_element_type=jnp.float32).astype(
        jnp.bfloat16
    )
    return lax.all_to_all(local_result, "grid", split_axis=0, concat_axis=1, tiled=True)


def solution(mesh):
    placed = (P(("grid", "band"), None), P())
    return jax.shard_map(
        body, mesh=mesh, in_specs=placed, out_specs=P(("grid", "band"), None), check_vma=False
    )
```

profile of v0, /device:TPU:480, one launch (start us, length us, event | category | flops | bytes accessed | tf_op | source)
XLA Modules:
  0.0 1096.2 jit_solution(2005917911756272368)
XLA Ops:
  6.5 13.6 %all-to-all-start = ((bf16[2,128,1024]{2,0,1:T(2,128)(2,1)}), bf16[2,128,1024]{2,0,1:T(2,128)(2,1)S(1)}, u32[]{:S(2)}, u32[]{:S(2)}) async-start(bf16[2,128,1024]{2,0,1:T(2,128)(2,1)} %bitcast.115), calls=%async_computation | async-start | bytes 1048576 | tf_op jit(solution)/shard_map/all_to_all | solution.py:40
  25.9 24.7 %all-to-all-done = bf16[2,128,1024]{2,0,1:T(2,128)(2,1)S(1)} async-done(((bf16[2,128,1024]{2,0,1:T(2,128)(2,1)}), bf16[2,128,1024]{2,0,1:T(2,128)(2,1)S(1)}, u32[]{:S(2)}, u32[]{:S(2)}) %all-to-all-start) | async-done | bytes 524320 | tf_op jit(solution)/shard_map/all_to_all | solution.py:40
  62.2 130.0 %all-gather.5.cloned.1.call-done = bf16[1024,1024]{1,0:T(8,128)(2,1)} async-done(((bf16[8,1024]{1,0:T(8,128)(2,1)}), bf16[1024,1024]{1,0:T(8,128)(2,1)}) %all-gather.5.cloned.1.call-update) | async-done | bytes 2097168 | tf_op jit(solution)/shard_map/all_gather | solution.py:57
  195.7 35.6 %all-gather.7.cloned.1.call-done = bf16[1024,1024]{1,0:T(8,128)(2,1)} async-done(((bf16[256,1024]{1,0:T(8,128)(2,1)}), bf16[1024,1024]{1,0:T(8,128)(2,1)}) %all-gather.7.cloned.1.call-update) | async-done | bytes 2097168 | tf_op jit(solution)/shard_map/all_gather | solution.py:63
  234.5 38.7 %all-gather.9.cloned.1.call-done = bf16[1024,1024]{1,0:T(8,128)(2,1)} async-done(((bf16[256,1024]{1,0:T(8,128)(2,1)}), bf16[1024,1024]{1,0:T(8,128)(2,1)}) %all-gather.9.cloned.1.call-update) | async-done | bytes 2097168 | tf_op jit(solution)/shard_map/all_gather | solution.py:67
  276.7 331.3 %all-reduce.3.cloned.1.call-done = f32[1024,256]{1,0:T(8,128)} async-done(((f32[1024,256]{1,0:T(8,128)}), f32[1024,256]{1,0:T(8,128)}) %all-reduce.3.cloned.1.call-update) | async-done | bytes 1048592 | tf_op jit(solution)/shard_map/psum | solution.py:72
  608.6 58.7 %all-gather.11.cloned.1.call-done = f32[1024,1024]{1,0:T(8,128)} async-done(((f32[1024,256]{1,0:T(8,128)}), f32[1024,1024]{1,0:T(8,128)}) %all-gather.11.cloned.1.call-update) | async-done | bytes 4194320 | tf_op jit(solution)/shard_map/all_gather | solution.py:73
  710.7 11.7 %cholesky.222 = f32[128,128]{1,0:T(8,128)S(1)} custom-call(f32[128,128]{1,0:T(8,128)S(1)} %cholesky.577), custom_call_target="Cholesky" | custom-call | tf_op jit(solution)/shard_map/jit(cholesky)/cholesky | solution.py:75
  724.9 9.8 custom-call.62
  738.7 11.7 %cholesky.243 = f32[128,128]{1,0:T(8,128)S(1)} custom-call(f32[128,128]{1,0:T(8,128)S(1)} %cholesky.581), custom_call_target="Cholesky" | custom-call | tf_op jit(solution)/shard_map/jit(cholesky)/cholesky | solution.py:75
  752.3 9.9 custom-call.63
  765.6 11.7 %cholesky.466 = f32[128,128]{1,0:T(8,128)S(1)} custom-call(f32[128,128]{1,0:T(8,128)S(1)} %cholesky.586), custom_call_target="Cholesky" | custom-call | tf_op jit(solution)/shard_map/jit(cholesky)/cholesky | solution.py:75
  778.6 9.8 custom-call.64
  792.0 11.9 %cholesky.485 = f32[128,128]{1,0:T(8,128)S(1)} custom-call(f32[128,128]{1,0:T(8,128)S(1)} %cholesky.591), custom_call_target="Cholesky" | custom-call | tf_op jit(solution)/shard_map/jit(cholesky)/cholesky | solution.py:75
  805.2 9.8 custom-call.65
  818.4 11.7 %cholesky.504 = f32[128,128]{1,0:T(8,128)S(1)} custom-call(f32[128,128]{1,0:T(8,128)S(1)} %cholesky.596), custom_call_target="Cholesky" | custom-call | tf_op jit(solution)/shard_map/jit(cholesky)/cholesky | solution.py:75
  831.5 9.8 custom-call.66
  845.0 11.7 %cholesky.524 = f32[128,128]{1,0:T(8,128)S(1)} custom-call(f32[128,128]{1,0:T(8,128)S(1)} %cholesky.601), custom_call_target="Cholesky" | custom-call | tf_op jit(solution)/shard_map/jit(cholesky)/cholesky | solution.py:75
  870.8 11.7 %cholesky.544 = f32[128,128]{1,0:T(8,128)S(1)} custom-call(f32[128,128]{1,0:T(8,128)S(1)} %cholesky.606), custom_call_target="Cholesky" | custom-call | tf_op jit(solution)/shard_map/jit(cholesky)/cholesky | solution.py:75
  883.8 10.0 custom-call.68
  896.4 11.7 %cholesky.562 = f32[128,128]{1,0:T(8,128)S(1)} custom-call(f32[128,128]{1,0:T(8,128)S(1)} %convolution_subtract_fusion.13), custom_call_target="Cholesky" | custom-call | tf_op jit(solution)/shard_map/jit(cholesky)/cholesky | solution.py:75
  919.1 23.0 %while.2 = (s32[]{:T(128)}, f32[1024,1024]{1,0:T(8,128)}, s32[8,2]{0,1:T(2,128)S(1)}, f32[8,128,128]{2,1,0:T(8,128)S(1)}, s32[]{:T(128)}) while((s32[]{:T(128)}, f32[1024,1024]{1,0:T(8,128)}, s32[8,2]{0,1:T(2,128)S(1)}, f32[8,128,128]{2,1,0:T(8,128)S(1)}, s32[]{:T(128)}) %tuple.49), condition=%wide.while_cond.1, body=%wide.while_body.1.sunk | while | flops 2 | bytes 131181 | solution.py:83
  942.1 78.8 %custom-call.69 = f32[8,128,128]{1,2,0:T(8,128)S(1)} custom-call(f32[8,128,128]{2,1,0:T(8,128)S(1)} %get-tuple-element.21), custom_call_target="InvertDiagBlocksLowerTriangular" | custom-call | tf_op jit(solution)/shard_map/triangular_solve | solution.py:83
  1042.6 46.1 %all_to_all.58 = bf16[128,2,1024]{2,1,0:T(2,128)(2,1)S(1)} all-to-all(bf16[128,2,1024]{2,1,0:T(2,128)(2,1)S(1)} %all_to_all.50), channel_id=1, replica_groups=mesh['grid'=128,'band'=4] {'grid'}, dimensions={0} | all-to-all | bytes 1048576 | tf_op jit(solution)/shard_map/all_to_all | solution.py:91
  (172 shorter events, 166.4 us)
Async XLA Ops:
  6.5 13.7 %copy-start = (s32[1024]{0:T(1024)S(1)}, s32[1024]{0:T(1024)}, u32[]{:S(2)}) copy-start(s32[1024]{0:T(1024)} %param.5) | copy-start | bytes 12292
  6.5 44.1 %all-to-all-start = ((bf16[2,128,1024]{2,0,1:T(2,128)(2,1)}), bf16[2,128,1024]{2,0,1:T(2,128)(2,1)S(1)}, u32[]{:S(2)}, u32[]{:S(2)}) async-start(bf16[2,128,1024]{2,0,1:T(2,128)(2,1)} %bitcast.115), calls=%async_computation | async-start | bytes 1048576 | tf_op jit(solution)/shard_map/all_to_all | solution.py:40
  20.2 172.1 %all-gather.5.cloned.1.call-start = ((), (), s32[]{:S(2)}) async-start(), calls=%async_computation.3 | async-start | bytes 2113536 | tf_op jit(solution)/shard_map/all_gather | solution.py:57
  50.9 10.6 copy-start.3
  61.4 169.9 %all-gather.7.cloned.1.call-start = ((), (), s32[]{:S(2)}) async-start(), calls=%async_computation.4 | async-start | bytes 2621440 | tf_op jit(solution)/shard_map/all_gather | solution.py:63
  62.1 211.1 %all-gather.9.cloned.1.call-start = ((), (), s32[]{:S(2)}) async-start(), calls=%async_computation.5 | async-start | bytes 2621440 | tf_op jit(solution)/shard_map/all_gather | solution.py:67
  234.5 373.6 %all-reduce.3.cloned.1.call-start = ((), (), s32[]{:S(2)}) async-start(), calls=%async_computation.6 | async-start | bytes 2097152 | tf_op jit(solution)/shard_map/psum | solution.py:72
  276.7 390.7 %all-gather.11.cloned.1.call-start = ((), (), s32[]{:S(2)}) async-start(), calls=%async_computation.7 | async-start | bytes 5242880 | tf_op jit(solution)/shard_map/all_gather | solution.py:73
  708.8 1.9 copy-start.2
  1020.9 10.8 copy-start.5
  1032.0 8.4 copy-start.4
  1035.5 54.0 %copy-start.1 = (s32[1024]{0:T(1024)S(1)}, s32[1024]{0:T(1024)}, u32[]{:S(2)}) copy-start(s32[1024]{0:T(1024)} %param.5) | copy-start | bytes 12292
Sparse Core Ops, SparseCore 0:
  61.5 130.7 all-gather.4
  194.4 36.9 all-gather.6
  234.6 38.5 all-gather.8
  276.8 331.2 all-reduce.2
  610.2 57.0 all-gather.10
where the time goes:
time: 1110 us; the launch traced here: 1100 us
  waiting for transfers between devices  620 us (56%)
  other arithmetic  271 us (24%)
  local copies, waits for them, and re-layouts  71.2 us (6%)
  blocking collectives  55.7 us (5%)
  matrix products  46 us (4%)
  between operations  19 us (2%)
  starting transfers between devices  13.8 us (1%)
    psum x1, waiting for transfers between devices, body(): gram_columns = lax.psum(local_columns, 'grid')  331 us
    another operation x31, other arithmetic, body(): factor = jnp.linalg.cholesky(gram)  173 us
    all_gather x1, waiting for transfers between devices, body(): arrived = lax.all_gather(sorted_slots, 'grid', axis=0, tiled=True)  130 us
    another operation x4, other arithmetic, body(): lax.linalg.triangular_solve(factor, unit_columns, left_side=True, lower=T...  83.6 us
    all_gather x1, waiting for transfers between devices, body(): gram_mixed = lax.all_gather(gram_columns, 'band', axis=1, tiled=True)  58.7 us
    all_to_all x1, blocking collectives, body(): lax.all_to_all(local_result, 'grid', split_axis=0, concat_axis=1, tiled=T...  46.1 us
    all_gather x1, waiting for transfers between devices, body(): gathered = lax.all_gather(products, 'band', axis=0, tiled=True)  38.7 us
    all_gather x1, waiting for transfers between devices, body(): slab = lax.all_gather(slab_own, 'band', axis=0, tiled=True)  35.6 us
  transfers between devices with their start and end apart: 6, of which 6 were waited for; matrix products, arithmetic and copies ran while one was open for 1% of the time, Pallas kernels for 0%

commit v1 on v0

v1 whole, which is shorter than its diff:
```python
import functools
import math

import jax
import jax.numpy as jnp
from jax import lax
from jax.experimental import pallas as pl
from jax.experimental.pallas import tpu as pltpu
from jax.sharding import PartitionSpec as P

MESH = pl.DeviceIdType.MESH
X, Y, Z, CORES = 4, 4, 16, 2
NB = 1024
BLOCK = 128
BLOCKS = NB // BLOCK
TILES = 576
OWNERS = 9
ROWS_OF_CORE = ((0, 3, 4, 7), (1, 2, 5, 6))
VMEM = 56 * 1024 * 1024


def place():
    grid = lax.axis_index("grid")
    return lax.axis_index("band"), lax.rem(grid // CORES, Y), grid // (CORES * Y), lax.rem(grid, CORES)


def device(x, y, z, core):
    return ((z * Y + y) * CORES + core, x)


def greet(x, y, z, core, plane):
    barrier = pltpu.get_barrier_semaphore()
    partners = [device(x, y, z, 1 - core)]
    for along_y in range(Y):
        for along_x in range(X):
            if (along_x or along_y) and (plane or not (along_x and along_y)):
                partners.append(device(lax.rem(x + along_x, X), lax.rem(y + along_y, Y), z, core))
    for step in range(1, Z):
        partners.append(device(x, y, lax.rem(z + step, Z), core))
    for partner in partners:
        pl.semaphore_signal(barrier, inc=1, device_id=partner, device_id_type=MESH)
    pl.semaphore_wait(barrier, len(partners))


def remote(src, dst, send, recv, target):
    return pltpu.make_async_remote_copy(
        src_ref=src, dst_ref=dst, send_sem=send, recv_sem=recv, device_id=target, device_id_type=MESH
    )


def spread(out, unit, x, y, z, core, send, recv):
    half = 16 * unit
    base = core * 2 * half
    firsts = (x, y)
    seconds = (y, x)

    def mate(axis_is_x, step):
        if axis_is_x:
            return device(lax.rem(x + step, X), y, z, core)
        return device(x, lax.rem(y + step, Y), z, core)

    started = []
    inner = []
    for h in range(2):
        mine = out.at[pl.ds(base + h * half + (firsts[h] * 4 + seconds[h]) * unit, unit)]
        for step in range(1, 4):
            copy = remote(mine, mine, send.at[0, h, step], recv.at[0, h, step], mate(h == 1, step))
            copy.start()
            inner.append(copy)
    for copy in inner:
        copy.wait_recv()
    started += inner
    sibling = device(x, y, z, 1 - core)
    across = []
    near = []
    block = 4 * unit

    def part(h, where, begin=0, size=block):
        return out.at[pl.ds(base + h * half + lax.rem(firsts[h] + where, 4) * block + begin, size)]

    def forward(h, index, ref):
        copy = remote(ref, ref, send.at[2, h, index], recv.at[2, h, index], sibling)
        copy.start()
        across.append(copy)

    for h in range(2):
        for index, step in ((0, 1), (1, 3)):
            copy = remote(part(h, 0), part(h, 0), send.at[1, h, index], recv.at[1, h, index], mate(h == 0, step))
            copy.start()
            near.append((h, index, step, copy))
    for h in range(2):
        forward(h, 0, part(h, 0))
    far = []
    for h, index, step, copy in near:
        copy.wait_recv()
        ref = part(h, 4 - step, index * (block // 2), block // 2)
        onward = remote(ref, ref, send.at[1, h, 2 + index], recv.at[1, h, 2 + index], mate(h == 0, step))
        onward.start()
        far.append(onward)
        forward(h, 1 + index, part(h, 4 - step))
        started.append(copy)
    for copy in far:
        copy.wait_recv()
    for h in range(2):
        forward(h, 3, part(h, 2))
    for copy in across:
        copy.wait_recv()
    for copy in started + far + across:
        copy.wait_send()


def order_of_z():
    steps = []
    for step in range(1, Z // 2 + 1):
        steps.append(step)
        if step != Z - step:
            steps.append(Z - step)
    return steps


class Regroup:
    def __init__(self, source, out, beside, landed, sems, spot):
        self.source, self.out, self.beside, self.landed = source, out, beside, landed
        self.p_send, self.p_recv, self.z_send, self.z_recv, self.y_send, self.y_recv, self.local = sems
        self.x, self.y, self.z, self.core = spot
        self.origin = (self.core, 1 - self.core)
        self.pair = remote(
            source.at[:, :, 1 - self.core], beside, self.p_send, self.p_recv,
            device(self.x, self.y, self.z, 1 - self.core),
        )
        self.done = []
        self.paths = []
        self.plane = []

    def leaving(self, path, z):
        return self.source.at[z, :, self.core] if path == 0 else self.beside.at[z]

    def start_z(self, path):
        x, y, z, core = self.x, self.y, self.z, self.core
        if path == 1:
            self.pair.wait_recv()
        landing = self.landed.at[self.origin[path], z]
        copies = []
        for step in order_of_z():
            target = lax.rem(z + step, Z)
            copy = remote(
                self.leaving(path, target), landing, self.z_send.at[path, step], self.z_recv.at[path, step],
                device(x, y, target, core),
            )
            copy.start()
            copies.append(copy)
        own = pltpu.make_async_copy(self.leaving(path, z), landing, self.local.at[path])
        own.start()
        self.paths.append((own, copies))

    def start_plane(self, path):
        x, y, z, core = self.x, self.y, self.z, self.core
        own, copies = self.paths[path]
        own.wait()
        for copy in copies:
            copy.wait_recv()
        self.done += copies
        origin = self.origin[path]
        landing = self.out.at[:, y, origin, x]
        for along_y in range(Y):
            for along_x in range(X):
                if along_x or along_y:
                    to_x, to_y = lax.rem(x + along_x, X), lax.rem(y + along_y, Y)
                    index = along_y * X + along_x
                    copy = remote(
                        self.landed.at[origin, :, to_y, to_x], landing,
                        self.y_send.at[path, index], self.y_recv.at[path, index],
                        device(to_x, to_y, z, core),
                    )
                    copy.start()
                    self.plane.append(copy)
        keep = pltpu.make_async_copy(self.landed.at[origin, :, y, x], landing, self.local.at[2 + path])
        keep.start()
        self.done_keep = getattr(self, "done_keep", []) + [keep]

    def finish(self):
        for copy in self.plane:
            copy.wait_recv()
        for keep in self.done_keep:
            keep.wait()
        for copy in self.plane + self.done + [self.pair]:
            copy.wait_send()


def regroup_scratch(points):
    return [
        pltpu.VMEM((Z, Y, X, 2, points), jnp.bfloat16),
        pltpu.VMEM((CORES, Z, Y, X, 2, points), jnp.bfloat16),
        pltpu.SemaphoreType.DMA,
        pltpu.SemaphoreType.DMA,
        pltpu.SemaphoreType.DMA((2, Z)),
        pltpu.SemaphoreType.DMA((2, Z)),
        pltpu.SemaphoreType.DMA((2, X * Y)),
        pltpu.SemaphoreType.DMA((2, X * Y)),
        pltpu.SemaphoreType.DMA((4,)),
    ]


def gather_kernel(orbitals, piece, slab, rows, beside, landed, *sems):
    moving, sems = sems[:7], sems[7:]
    q_send, q_recv, send, recv = sems
    x, y, z, core = place()
    greet(x, y, z, core, True)
    regroup = Regroup(orbitals, slab, beside, landed, moving, (x, y, z, core))
    regroup.pair.start()
    first = []
    for step in order_of_z():
        copy = remote(
            piece, rows.at[z, y, core, x], q_send.at[step], q_recv.at[step], device(x, y, lax.rem(z + step, Z), core)
        )
        copy.start()
        first.append(copy)
    regroup.start_z(0)
    regroup.start_z(1)
    rows[z, y, core, x] = piece[...]
    for copy in first:
        copy.wait_recv()
    second = []
    mine = rows.at[:, y, core, x]
    for step in range(1, Y):
        copy = remote(
            mine, mine, send.at[0, step], recv.at[0, step], device(x, lax.rem(y + step, Y), z, core)
        )
        copy.start()
        second.append(copy)
    for copy in second:
        copy.wait_recv()
    sibling = device(x, y, z, 1 - core)
    near, far, last = [], [], []

    def along_x(step):
        return device(lax.rem(x + step, X), y, z, core)

    def forward(index, ref):
        copy = remote(ref, ref, send.at[2, index], recv.at[2, index], sibling)
        copy.start()
        last.append(copy)

    mine = rows.at[:, :, core, x]
    for index, step in ((0, 1), (1, 3)):
        copy = remote(mine, mine, send.at[1, index], recv.at[1, index], along_x(step))
        copy.start()
        near.append(copy)
    forward(0, mine)
    for index, step in ((0, 1), (1, 3)):
        near[index].wait_recv()
        source = lax.rem(x + 4 - step, X)
        ref = rows.at[pl.ds(index * (Z // 2), Z // 2), :, core, source]
        copy = remote(ref, ref, send.at[1, 2 + index], recv.at[1, 2 + index], along_x(step))
        copy.start()
        far.append(copy)
        forward(1 + index, rows.at[:, :, core, source])
    regroup.start_plane(0)
    for copy in far:
        copy.wait_recv()
    forward(3, rows.at[:, :, core, lax.rem(x + 2, X)])
    regroup.start_plane(1)
    for copy in last:
        copy.wait_recv()
    regroup.finish()
    for copy in first + second + near + far + last:
        copy.wait_send()


def gather(orbitals, piece):
    points = orbitals.shape[-1]
    return pl.pallas_call(
        gather_kernel,
        out_shape=[
            jax.ShapeDtypeStruct((Z, Y, CORES, X, 2, points), jnp.bfloat16),
            jax.ShapeDtypeStruct((Z, Y, CORES, X, 16, 128), jnp.bfloat16),
        ],
        in_specs=[pl.BlockSpec(memory_space=pltpu.VMEM)] * 2,
        out_specs=[pl.BlockSpec(memory_space=pltpu.VMEM)] * 2,
        scratch_shapes=regroup_scratch(points) + [
            pltpu.SemaphoreType.DMA((Z,)),
            pltpu.SemaphoreType.DMA((Z,)),
            pltpu.SemaphoreType.DMA((3, 4)),
            pltpu.SemaphoreType.DMA((3, 4)),
        ],
        compiler_params=pltpu.CompilerParams(
            collective_id=0, has_side_effects=True, vmem_limit_bytes=32 * 1024 * 1024
        ),
        name="gather_slab_and_pivot_rows",
    )(orbitals, piece)


def return_kernel(local, out, beside, landed, *sems):
    x, y, z, core = place()
    greet(x, y, z, core, True)
    regroup = Regroup(local, out, beside, landed, sems, (x, y, z, core))
    regroup.pair.start()
    regroup.start_z(0)
    regroup.start_z(1)
    regroup.start_plane(0)
    regroup.start_plane(1)
    regroup.finish()


def give_back(local):
    points = local.shape[-1]
    return pl.pallas_call(
        return_kernel,
        out_shape=jax.ShapeDtypeStruct(local.shape, jnp.bfloat16),
        in_specs=[pl.BlockSpec(memory_space=pltpu.VMEM)],
        out_specs=pl.BlockSpec(memory_space=pltpu.VMEM),
        scratch_shapes=regroup_scratch(points),
        compiler_params=pltpu.CompilerParams(
            collective_id=2, has_side_effects=True, vmem_limit_bytes=32 * 1024 * 1024
        ),
        name="return_localized",
    )(local)


def gram_kernel(products, out, theirs, terms, got0, got1, got2, got3, send, recv, r_send, r_recv, z_send, z_recv, g_send, g_recv, p_send, p_recv):
    x, y, z, core = place()
    greet(x, y, z, core, False)
    pair = remote(products, theirs, p_send, p_recv, device(x, y, z, 1 - core))
    pair.start()
    pair.wait_recv()
    contract = (((1,), (1,)), ((), ()))

    for which in range(CORES):

        @pl.when(core == which)
        def _():
            count = 0
            for i in ROWS_OF_CORE[which]:
                rows = slice(i * BLOCK, (i + 1) * BLOCK)
                rest = slice(i * BLOCK, NB)
                row = lax.dot_general(
                    products[rows, :], products[rest, :], contract, preferred_element_type=jnp.float32
                ) + lax.dot_general(
                    theirs[rows, :], theirs[rest, :], contract, preferred_element_type=jnp.float32
                )
                for j in range(BLOCKS - i):
                    terms[count * 16:(count + 1) * 16] = row[:, j * BLOCK:(j + 1) * BLOCK].reshape(16, 8, 128)
                    count += 1

    unit = OWNERS
    half = 16 * unit
    firsts = (x, y)
    seconds = (y, x)

    def mate(axis_is_x, step):
        if axis_is_x:
            return device(lax.rem(x + step, X), y, z, core)
        return device(x, lax.rem(y + step, Y), z, core)

    block = 4 * unit
    middle = block // 2

    def span(h, where, begin=0, size=block):
        return pl.ds(h * half + lax.rem(firsts[h] + where, 4) * block + begin, size)

    copies = []
    for h in range(2):
        for index, step in ((0, 1), (1, 3)):
            copy = remote(
                terms.at[span(h, 2, index * middle, middle)], got0.at[h, index],
                r_send.at[0, h, index], r_recv.at[0, h, index], mate(h == 0, step),
            )
            copy.start()
            copies.append((h, index, step, copy))
    near = []
    for h, index, step, copy in copies:
        copy.wait_recv()
        part = span(h, step, index * middle, middle)
        terms[part] = terms[part] + got0[h, index]
        onward = remote(
            terms.at[span(h, step)], got1.at[h, index], r_send.at[2, h, index], r_recv.at[2, h, index],
            mate(h == 0, step),
        )
        onward.start()
        near.append(onward)
    copies = [copy for _, _, _, copy in copies] + near
    for copy in near:
        copy.wait_recv()
    for h in range(2):
        mine = span(h, 0)
        terms[mine] = terms[mine] + (got1[h, 0] + got1[h, 1])
    later = []
    for step in range(1, 4):
        for h in range(2):
            target = lax.rem(seconds[h] + step, 4)
            copy = remote(
                terms.at[pl.ds(h * half + (firsts[h] * 4 + target) * unit, unit)],
                got2.at[h, step - 1],
                r_send.at[1, h, step],
                r_recv.at[1, h, step],
                mate(h == 1, step),
            )
            copy.start()
            later.append(copy)
    for copy in later:
        copy.wait_recv()
    starts = [h * half + (firsts[h] * 4 + seconds[h]) * unit for h in range(2)]
    for h in range(2):
        mine = pl.ds(starts[h], unit)
        terms[mine] = terms[mine] + (got2[h, 0] + got2[h, 1]) + got2[h, 2]

    def to_owner(step, h):
        target = lax.rem(z + step, Z)
        tile = jnp.minimum(target, OWNERS - 1)
        return target, remote(
            terms.at[starts[h] + tile],
            got3.at[step - 1, h],
            z_send.at[step, h],
            z_recv.at[step, h],
            device(x, y, target, core),
        )

    for step in range(1, Z):
        for h in range(2):
            target, copy = to_owner(step, h)

            @pl.when(target < OWNERS)
            def _():
                copy.start()

    goals = [core * 2 * half + starts[h] for h in range(2)]
    tile = jnp.minimum(z, OWNERS - 1)

    def to_all(step, h):
        return remote(
            out.at[goals[h] + tile],
            out.at[goals[h] + tile],
            g_send.at[step, h],
            g_recv.at[step, h],
            device(x, y, lax.rem(z + step, Z), core),
        )

    @pl.when(z < OWNERS)
    def _():
        for step in range(1, Z):
            for h in range(2):
                to_owner(step, h)[1].wait_recv()
        for h in range(2):
            total = terms[starts[h] + tile]
            for step in range(1, Z):
                total = total + got3[step - 1, h]
            out[goals[h] + tile] = total
        for step in range(1, Z):
            for h in range(2):
                to_all(step, h).start()

    for step in range(1, Z):
        source = lax.rem(z + Z - step, Z)

        @pl.when(source < OWNERS)
        def _():
            for h in range(2):
                to_all(step, h).wait_recv()

    spread(out, unit, x, y, z, core, send, recv)

    for step in range(1, Z):
        for h in range(2):
            target, copy = to_owner(step, h)

            @pl.when(target < OWNERS)
            def _():
                copy.wait_send()

    @pl.when(z < OWNERS)
    def _():
        for step in range(1, Z):
            for h in range(2):
                to_all(step, h).wait_send()

    for copy in copies + later:
        copy.wait_send()
    pair.wait_send()


def sum_gram(products):
    unit = OWNERS
    return pl.pallas_call(
        gram_kernel,
        out_shape=jax.ShapeDtypeStruct((TILES, 8, 128), jnp.float32),
        in_specs=[pl.BlockSpec(memory_space=pltpu.VMEM)],
        out_specs=pl.BlockSpec(memory_space=pltpu.VMEM),
        scratch_shapes=[
            pltpu.VMEM(products.shape, jnp.bfloat16),
            pltpu.VMEM((TILES // 2, 8, 128), jnp.float32),
            pltpu.VMEM((2, 2, 2 * unit, 8, 128), jnp.float32),
            pltpu.VMEM((2, 2, 4 * unit, 8, 128), jnp.float32),
            pltpu.VMEM((2, 3, unit, 8, 128), jnp.float32),
            pltpu.VMEM((Z - 1, 2, 8, 128), jnp.float32),
            pltpu.SemaphoreType.DMA((3, 2, 4)),
            pltpu.SemaphoreType.DMA((3, 2, 4)),
            pltpu.SemaphoreType.DMA((3, 2, 4)),
            pltpu.SemaphoreType.DMA((3, 2, 4)),
            pltpu.SemaphoreType.DMA((Z, 2)),
            pltpu.SemaphoreType.DMA((Z, 2)),
            pltpu.SemaphoreType.DMA((Z, 2)),
            pltpu.SemaphoreType.DMA((Z, 2)),
            pltpu.SemaphoreType.DMA,
            pltpu.SemaphoreType.DMA,
        ],
        compiler_params=pltpu.CompilerParams(
            collective_id=1, has_side_effects=True, vmem_limit_bytes=32 * 1024 * 1024
        ),
        name="sum_gram",
    )(products)


def split(value):
    high = value.astype(jnp.bfloat16)
    return high, (value - high.astype(jnp.float32)).astype(jnp.bfloat16)


def dot(a, b):
    return jnp.dot(a, b, preferred_element_type=jnp.float32)


def factor_block(load, lane, row):
    full = (8, 128)
    groups = [load(g) for g in range(16)]
    for quarter in range(4):
        first = 4 * quarter
        for g in range(first, first + 4):
            at = 8 * g
            panel = groups[g]
            columns = [jnp.broadcast_to(panel[:, at + t:at + t + 1], full) for t in range(8)]
            a = [[jnp.broadcast_to(columns[t][i:i + 1, :], full) for t in range(i + 1)] for i in range(8)]
            below = [[None] * 8 for _ in range(8)]
            scale = []
            for s in range(8):
                r = lax.rsqrt(a[s][s])
                scale.append(r)
                for i in range(s + 1, 8):
                    below[i][s] = a[i][s] * r
                for i in range(s + 1, 8):
                    for t in range(s + 1, i + 1):
                        a[i][t] = a[i][t] - below[i][s] * below[t][s]
            inside = (lane >= at) & (lane < at + 8)
            panel = jnp.where(inside, (lane == row + at).astype(jnp.float32), panel)
            solved = []
            for s in range(8):
                value = jnp.broadcast_to(panel[s:s + 1, :], full)
                for t in range(s):
                    value = value - below[s][t] * solved[t]
                solved.append(value * scale[s])
            result = solved[0]
            for s in range(1, 8):
                result = jnp.where(row == s, solved[s], result)
            groups[g] = result
            for other in range(g + 1, first + 4):
                target = groups[other]
                left = []
                for s in range(8):
                    value = jnp.broadcast_to(target[:, at + s:at + s + 1], full)
                    for t in range(s):
                        value = value - below[s][t] * left[t]
                    left.append(value * scale[s])
                target = jnp.where(inside, 0.0, target)
                for s in range(8):
                    target = target - left[s] * solved[s]
                groups[other] = target
        if quarter < 3:
            at = 32 * quarter
            inside = (lane >= at) & (lane < at + 32)
            rows = jnp.concatenate(
                [
                    jnp.where(inside & (lane > 8 * g + row), 0.0, groups[g])
                    for g in range(first, first + 4)
                ],
                axis=0,
            )
            turned = rows.T[at + 32:, :]
            high, low = split(rows)
            turned_high, turned_low = split(turned)
            change = dot(turned_high, high) + dot(turned_low, high) + dot(turned_high, low)
            for other in range(first + 4, 16):
                begin = (other - first - 4) * 8
                groups[other] = jnp.where(inside, 0.0, groups[other]) - change[begin:begin + 8, :]
    return [jnp.where(lane > 8 * g + row, 0.0, groups[g]) for g in range(16)]


def solve_kernel(gram, products, out, mat, inverse):
    lane = lax.broadcasted_iota(jnp.int32, (8, 128), 1)
    row = lax.broadcasted_iota(jnp.int32, (8, 128), 0)
    count = 0
    for rows in ROWS_OF_CORE:
        for i in rows:
            for j in range(i, BLOCKS):
                mat[i * BLOCK:(i + 1) * BLOCK, j * BLOCK:(j + 1) * BLOCK] = (
                    gram[count * 16:(count + 1) * 16].reshape(BLOCK, BLOCK) / 131072.0
                )
                count += 1
            if i:
                mat[i * BLOCK:(i + 1) * BLOCK, :i * BLOCK] = jnp.zeros((BLOCK, i * BLOCK), jnp.float32)

    def step(k, carry):
        begin = pl.multiple_of(k * BLOCK, BLOCK)
        own = pl.ds(begin, BLOCK)

        def load(g):
            return mat[pl.ds(pl.multiple_of(begin + 8 * g, 8), 8), own]

        for g, value in enumerate(factor_block(load, lane, row)):
            mat[pl.ds(pl.multiple_of(begin + 8 * g, 8), 8), own] = value
        for kk in range(BLOCKS):

            @pl.when(k == kk)
            def _():
                at = kk * BLOCK
                high, low = split(mat[at:at + BLOCK, at:at + BLOCK])
                left = jnp.concatenate([high, low], axis=1)
                spans = [(0, at), (at + BLOCK, NB)]
                for start, stop in spans:
                    if start < stop:
                        up, down = split(mat[at:at + BLOCK, start:stop])
                        mat[at:at + BLOCK, start:stop] = dot(left, jnp.concatenate([up, up], axis=0)) + dot(high, down)
                if kk + 1 < BLOCKS:
                    after = at + BLOCK
                    turned_high, turned_low = split(mat[at:at + BLOCK, after:].T)
                    turned = jnp.concatenate([turned_high, turned_low], axis=1)
                    for start in range(0, NB, 256):
                        up, down = split(mat[at:at + BLOCK, start:start + 256])
                        change = dot(turned, jnp.concatenate([up, up], axis=0)) + dot(turned_high, down)
                        if start <= at < start + 256:
                            for part in (start, start + BLOCK):
                                piece = change[:, part - start:part - start + BLOCK]
                                if part == at:
                                    mat[after:, part:part + BLOCK] = -piece
                                else:
                                    mat[after:, part:part + BLOCK] = mat[after:, part:part + BLOCK] - piece
                        else:
                            mat[after:, start:start + 256] = mat[after:, start:start + 256] - change

        return carry

    lax.fori_loop(0, BLOCKS, step, 0)
    for i in range(BLOCKS):
        at = i * BLOCK
        inverse[at:at + BLOCK, :at + BLOCK] = mat[at:at + BLOCK, :at + BLOCK].astype(jnp.bfloat16)
    for i in range(BLOCKS):
        at = i * BLOCK
        out[at:at + BLOCK, :] = dot(
            inverse[at:at + BLOCK, :at + BLOCK], products[:at + BLOCK, :]
        ).astype(jnp.bfloat16)


def solve(gram, products):
    return pl.pallas_call(
        solve_kernel,
        out_shape=jax.ShapeDtypeStruct(products.shape, jnp.bfloat16),
        in_specs=[pl.BlockSpec(memory_space=pltpu.VMEM)] * 2,
        out_specs=pl.BlockSpec(memory_space=pltpu.VMEM),
        scratch_shapes=[pltpu.VMEM((NB, NB), jnp.float32), pltpu.VMEM((NB, NB), jnp.bfloat16)],
        compiler_params=pltpu.CompilerParams(vmem_limit_bytes=VMEM),
        name="factor_and_localize",
    )(gram, products)


def pick(orbitals, pivots):
    folded = orbitals.reshape(2, 1024, 128)
    outer = (pivots[:, None] // 128 == jnp.arange(1024, dtype=jnp.int32)[None, :]).astype(jnp.bfloat16)
    inner = pivots[:, None] % 128 == jnp.arange(128, dtype=jnp.int32)[None, :]
    rows = jnp.einsum("jh,rhl->rjl", outer, folded, preferred_element_type=jnp.float32)
    return jnp.sum(jnp.where(inner[None], rows, 0.0), axis=2).astype(jnp.bfloat16)


def body(orbitals, pivots):
    points = orbitals.shape[1] // 512
    entries = (Z, Y, CORES, X, 2, points)
    piece = pick(orbitals, pivots).reshape(16, 128)
    outgoing = orbitals.reshape(2, 512, points).transpose(1, 0, 2).reshape(entries)
    slab, rows = gather(outgoing, piece)
    products = (
        lax.dot_general(
            rows.reshape(NB, NB), slab.reshape(NB, points), (((0,), (0,)), ((), ())),
            preferred_element_type=jnp.float32,
        )
        * (1.0 / math.sqrt(NB))
    ).astype(jnp.bfloat16)
    gram = sum_gram(products)
    local = solve(gram, products)
    returned = give_back(local.reshape(entries))
    return returned.reshape(512, 2, points).transpose(1, 0, 2).reshape(orbitals.shape)


def solution(mesh):
    placed = (P(("grid", "band"), None), P())
    return jax.shard_map(
        body, mesh=mesh, in_specs=placed, out_specs=P(("grid", "band"), None), check_vma=False
    )
```

time: 1110 us -> 210 us (0.19)
  the two profiles are of different devices: /device:TPU:480 before, /device:TPU:2 now
where the time goes in v1:
time: 210 us
  Pallas kernels  198 us (94%)
  local copies, waits for them, and re-layouts  7.34 us (3%)
  matrix products  3.53 us (2%)
    pallas_call x1, Pallas kernels, sum_gram(): pl.pallas_call(gram_kernel, out_shape=jax.ShapeDtypeStruct((TILES, 8, 128...  61.6 us
    pallas_call x1, Pallas kernels, gather(): pl.pallas_call(gather_kernel, out_shape=[jax.ShapeDtypeStruct((Z, Y, CORE...  51.9 us
    pallas_call x1, Pallas kernels, give_back(): pl.pallas_call(return_kernel, out_shape=jax.ShapeDtypeStruct(local.shape,...  42.4 us
    pallas_call x1, Pallas kernels, solve(): pl.pallas_call(solve_kernel, out_shape=jax.ShapeDtypeStruct(products.shap...  42.2 us

profile of v1, /device:TPU:2, one launch (start us, length us, event | category | flops | bytes accessed | tf_op | source)
XLA Modules:
  0.0 209.8 jit_solution(9253319665981303103)
XLA Ops:
  0.0 0.7 add_select_fusion
  0.7 0.0 copy-start.1
  0.7 0.1 iota_compare_fusion.2
  0.8 1.2 copy.8
  1.9 0.2 copy.4
  2.2 1.2 select_reduce_fusion
  3.4 0.0 copy-done.1
  3.4 51.9 %gather_slab_and_pivot_rows.1 = (bf16[16,4,2,4,2,256]{5,4,3,2,1,0:T(2,128)(2,1)S(1)}, bf16[16,4,2,4,16,128]{5,4,3,2,1,0:T(8,128)(2,1)S(1)}) custom-call(bf16[16,4,2,4,2,256]{5,4,3,2,1,0:T(2,128)(2,1)S(1)} %bitcast.28, bf16[16,128]{1,0:T(8,128)(2,1)S(1)} %convert_element_type.16.piece), custom_call_target="tpu_custom_call" | custom-call | tf_op jit(solution)/shard_map/gather_slab_and_pivot_rows/pallas_call | solution.py:272
  55.3 2.3 %reshape.73 = bf16[1024,1024]{1,0:T(8,128)(2,1)} reshape(bf16[16,4,2,4,16,128]{5,4,3,2,1,0:T(8,128)(2,1)S(1)} %get-tuple-element.7) | data formatting | bytes 4194304 | tf_op jit(solution)/shard_map/reshape | solution.py:679
  57.6 0.2 reshape.74
  57.8 2.4 %fusion.2.products = bf16[1024,256]{1,0:T(8,128)(2,1)S(1)} fusion(bf16[1024,1024]{1,0:T(8,128)(2,1)} %reshape.73, bf16[1024,256]{1,0:T(8,128)(2,1)S(1)} %reshape.74), kind=kOutput, calls=%fused_computation.4 | convolution fusion | flops 537395200 | bytes 3145728 | tf_op jit(solution)/shard_map/dot_general | solution.py:678
  60.2 0.0 copy-start.2
  60.2 61.6 %sum_gram.1.gram = f32[576,8,128]{2,1,0:T(8,128)S(1)} custom-call(bf16[1024,256]{1,0:T(8,128)(2,1)S(1)} %fusion.2.products), custom_call_target="tpu_custom_call" | custom-call | tf_op jit(solution)/shard_map/sum_gram/pallas_call | solution.py:483
  121.8 0.0 copy-done.2
  121.8 0.0 copy-start
  121.8 1.4 copy-done
  123.2 42.2 %factor_and_localize.1 = bf16[1024,256]{1,0:T(8,128)(2,1)} custom-call(f32[576,8,128]{2,1,0:T(8,128)} %copy-done, bf16[1024,256]{1,0:T(8,128)(2,1)} %copy-done.2), custom_call_target="tpu_custom_call" | custom-call | tf_op jit(solution)/shard_map/factor_and_localize/pallas_call | solution.py:652
  165.4 1.2 reshape.75.local
  166.7 42.4 %return_localized.1 = bf16[16,4,2,4,2,256]{5,4,3,2,1,0:T(2,128)(2,1)S(1)} custom-call(bf16[16,4,2,4,2,256]{5,4,3,2,1,0:T(2,128)(2,1)S(1)} %reshape.75.local), custom_call_target="tpu_custom_call" | custom-call | tf_op jit(solution)/shard_map/return_localized/pallas_call | solution.py:307
  209.0 0.8 copy.10
  (1 shorter events, 0.0 us)
Async XLA Ops:
  0.7 2.7 %copy-start.1 = (bf16[2,131072]{1,0:T(2,128)(2,1)S(1)}, bf16[2,131072]{1,0:T(2,128)(2,1)}, u32[]{:S(2)}) copy-start(bf16[2,131072]{1,0:T(2,128)(2,1)} %param.2) | copy-start | bytes 1572868
  60.2 61.6 %copy-start.2 = (bf16[1024,256]{1,0:T(8,128)(2,1)}, bf16[1024,256]{1,0:T(8,128)(2,1)S(1)}, u32[]{:S(2)}) copy-start(bf16[1024,256]{1,0:T(8,128)(2,1)S(1)} %fusion.2.products) | copy-start | bytes 1572868
  121.8 1.4 copy-start

commit v2 on v1

--- a/solution.py
+++ b/solution.py
@@ -290,34 +290,51 @@
     )(orbitals, piece)
 
 
-def return_kernel(local, out, beside, landed, *sems):
+def return_kernel(landed, out, send, recv, kept):
     x, y, z, core = place()
-    greet(x, y, z, core, True)
-    regroup = Regroup(local, out, beside, landed, sems, (x, y, z, core))
-    regroup.pair.start()
-    regroup.start_z(0)
-    regroup.start_z(1)
-    regroup.start_plane(0)
-    regroup.start_plane(1)
-    regroup.finish()
-
-
-def give_back(local):
-    points = local.shape[-1]
+    barrier = pltpu.get_barrier_semaphore()
+    partners = []
+    for along_y in range(Y):
+        for along_x in range(X):
+            if along_x or along_y:
+                partners.append((lax.rem(x + along_x, X), lax.rem(y + along_y, Y), along_y * X + along_x))
+    for to_x, to_y, _ in partners:
+        pl.semaphore_signal(barrier, inc=1, device_id=device(to_x, to_y, z, core), device_id_type=MESH)
+    pl.semaphore_wait(barrier, len(partners))
+    landing = out.at[:, y, :, x]
+    copies = []
+    for to_x, to_y, index in partners:
+        copy = remote(
+            landed.at[:, :, to_y, to_x], landing, send.at[index], recv.at[index], device(to_x, to_y, z, core)
+        )
+        copy.start()
+        copies.append(copy)
+    keep = pltpu.make_async_copy(landed.at[:, :, y, x], landing, kept)
+    keep.start()
+    keep.wait()
+    for copy in copies:
+        copy.wait_recv()
+    for copy in copies:
+        copy.wait_send()
+
+
+def give_back(landed):
+    points = landed.shape[-1]
+    dma = pltpu.SemaphoreType.DMA
     return pl.pallas_call(
         return_kernel,
-        out_shape=jax.ShapeDtypeStruct(local.shape, jnp.bfloat16),
+        out_shape=jax.ShapeDtypeStruct((Z, Y, CORES, X, 2, points), jnp.bfloat16),
         in_specs=[pl.BlockSpec(memory_space=pltpu.VMEM)],
         out_specs=pl.BlockSpec(memory_space=pltpu.VMEM),
-        scratch_shapes=regroup_scratch(points),
+        scratch_shapes=[dma((X * Y,)), dma((X * Y,)), dma],
         compiler_params=pltpu.CompilerParams(
-            collective_id=2, has_side_effects=True, vmem_limit_bytes=32 * 1024 * 1024
+            collective_id=2, has_side_effects=True, vmem_limit_bytes=16 * 1024 * 1024
         ),
         name="return_localized",
-    )(local)
-
-
-def gram_kernel(products, out, theirs, terms, got0, got1, got2, got3, send, recv, r_send, r_recv, z_send, z_recv, g_send, g_recv, p_send, p_recv):
+    )(landed)
+
+
+def gram_kernel(products, landed, out, theirs, terms, got0, got1, got2, got3, mat, ready, beside, send, recv, r_send, r_recv, z_send, z_recv, g_send, g_recv, p_send, p_recv, *leave):
     x, y, z, core = place()
     greet(x, y, z, core, False)
     pair = remote(products, theirs, p_send, p_recv, device(x, y, z, 1 - core))
@@ -476,37 +493,47 @@
     for copy in copies + later:
         copy.wait_send()
     pair.wait_send()
-
-
-def sum_gram(products):
+    solve(out, products, landed, mat, ready, beside, leave, (x, y, z, core))
+
+
+def localize(products):
     unit = OWNERS
+    points = products.shape[1]
+    dma = pltpu.SemaphoreType.DMA
     return pl.pallas_call(
         gram_kernel,
-        out_shape=jax.ShapeDtypeStruct((TILES, 8, 128), jnp.float32),
+        out_shape=jax.ShapeDtypeStruct((Z, CORES, Y * X * 2, points), jnp.bfloat16),
         in_specs=[pl.BlockSpec(memory_space=pltpu.VMEM)],
         out_specs=pl.BlockSpec(memory_space=pltpu.VMEM),
         scratch_shapes=[
+            pltpu.VMEM((TILES, 8, 128), jnp.float32),
             pltpu.VMEM(products.shape, jnp.bfloat16),
             pltpu.VMEM((TILES // 2, 8, 128), jnp.float32),
             pltpu.VMEM((2, 2, 2 * unit, 8, 128), jnp.float32),
             pltpu.VMEM((2, 2, 4 * unit, 8, 128), jnp.float32),
             pltpu.VMEM((2, 3, unit, 8, 128), jnp.float32),
             pltpu.VMEM((Z - 1, 2, 8, 128), jnp.float32),
-            pltpu.SemaphoreType.DMA((3, 2, 4)),
-            pltpu.SemaphoreType.DMA((3, 2, 4)),
-            pltpu.SemaphoreType.DMA((3, 2, 4)),
-            pltpu.SemaphoreType.DMA((3, 2, 4)),
-            pltpu.SemaphoreType.DMA((Z, 2)),
-            pltpu.SemaphoreType.DMA((Z, 2)),
-            pltpu.SemaphoreType.DMA((Z, 2)),
-            pltpu.SemaphoreType.DMA((Z, 2)),
-            pltpu.SemaphoreType.DMA,
-            pltpu.SemaphoreType.DMA,
+            pltpu.VMEM((NB, NB), jnp.float32),
+            pltpu.VMEM((BLOCKS, CORES, 2, Y * X * 2, points), jnp.bfloat16),
+            pltpu.VMEM((BLOCKS, 2, Y * X * 2, points), jnp.bfloat16),
+            dma((3, 2, 4)),
+            dma((3, 2, 4)),
+            dma((3, 2, 4)),
+            dma((3, 2, 4)),
+            dma((Z, 2)),
+            dma((Z, 2)),
+            dma((Z, 2)),
+            dma((Z, 2)),
+            dma,
+            dma,
+            dma((BLOCKS,)),
+            dma((BLOCKS,)),
+            dma((2, Z)),
+            dma((2, Z)),
+            dma((2,)),
         ],
-        compiler_params=pltpu.CompilerParams(
-            collective_id=1, has_side_effects=True, vmem_limit_bytes=32 * 1024 * 1024
-        ),
-        name="sum_gram",
+        compiler_params=pltpu.CompilerParams(collective_id=1, has_side_effects=True, vmem_limit_bytes=VMEM),
+        name="sum_factor_and_localize",
     )(products)
 
 
@@ -583,7 +610,74 @@
     return [jnp.where(lane > 8 * g + row, 0.0, groups[g]) for g in range(16)]
 
 
-def solve_kernel(gram, products, out, mat, inverse):
+class Leave:
+    def __init__(self, ready, beside, landed, sems, spot):
+        self.ready, self.beside, self.landed = ready, beside, landed
+        self.p_send, self.p_recv, self.z_send, self.z_recv, self.local = sems
+        self.x, self.y, self.z, self.core = spot
+
+    def pair(self, k):
+        return remote(
+            self.ready.at[k, 1 - self.core], self.beside.at[k], self.p_send.at[k], self.p_recv.at[k],
+            device(self.x, self.y, self.z, 1 - self.core),
+        )
+
+    def source(self, path, k, part):
+        return self.ready.at[k, self.core, part] if path == 0 else self.beside.at[k, part]
+
+    def origin(self, path):
+        return self.core if path == 0 else 1 - self.core
+
+    def along(self, path, k, part):
+        return remote(
+            self.source(path, k, part), self.landed.at[self.z, self.origin(path)],
+            self.z_send.at[path, 2 * k + part], self.z_recv.at[path, self.z],
+            device(self.x, self.y, 2 * k + part, self.core),
+        )
+
+    def keep(self, path, k, part):
+        return pltpu.make_async_copy(
+            self.source(path, k, part), self.landed.at[self.z, self.origin(path)], self.local.at[path]
+        )
+
+    def start(self, path, k):
+        if path == 1:
+            self.pair(k).wait_recv()
+        for part in range(2):
+
+            @pl.when(self.z != 2 * k + part)
+            def _():
+                self.along(path, k, part).start()
+
+            @pl.when(self.z == 2 * k + part)
+            def _():
+                self.keep(path, k, part).start()
+
+    def finish(self):
+        for path in range(2):
+            for step in range(1, Z):
+                source = lax.rem(self.z + step, Z)
+                spot = self.landed.at[source, self.origin(path)]
+                remote(
+                    spot, spot, self.z_send.at[path, source], self.z_recv.at[path, source],
+                    device(self.x, self.y, source, self.core),
+                ).wait_recv()
+            for k in range(BLOCKS):
+                for part in range(2):
+
+                    @pl.when(self.z != 2 * k + part)
+                    def _():
+                        self.along(path, k, part).wait_send()
+
+                    @pl.when(self.z == 2 * k + part)
+                    def _():
+                        self.keep(path, k, part).wait()
+        for k in range(BLOCKS):
+            self.pair(k).wait_send()
+
+
+def solve(gram, products, landed, mat, ready, beside, sems, spot):
+    leave = Leave(ready, beside, landed, sems, spot)
     lane = lax.broadcasted_iota(jnp.int32, (8, 128), 1)
     row = lax.broadcasted_iota(jnp.int32, (8, 128), 0)
     count = 0
@@ -591,7 +685,7 @@
         for i in rows:
             for j in range(i, BLOCKS):
                 mat[i * BLOCK:(i + 1) * BLOCK, j * BLOCK:(j + 1) * BLOCK] = (
-                    gram[count * 16:(count + 1) * 16].reshape(BLOCK, BLOCK) / 131072.0
+                    gram[count * 16:(count + 1) * 16].reshape(BLOCK, BLOCK) * (1.0 / 131072.0)
                 )
                 count += 1
             if i:
@@ -618,6 +712,22 @@
                     if start < stop:
                         up, down = split(mat[at:at + BLOCK, start:stop])
                         mat[at:at + BLOCK, start:stop] = dot(left, jnp.concatenate([up, up], axis=0)) + dot(high, down)
+                inverse = jnp.concatenate(
+                    [
+                        mat[at + 64 * to_z + 16 * to_y + 8 * to_core:at + 64 * to_z + 16 * to_y + 8 * to_core + 8, :at + BLOCK]
+                        for to_core in range(CORES)
+                        for to_z in range(2)
+                        for to_y in range(Y)
+                    ],
+                    axis=0,
+                ).astype(jnp.bfloat16)
+                local = dot(inverse, products[:at + BLOCK, :]).astype(jnp.bfloat16)
+                for to_core in range(CORES):
+                    for to_z in range(2):
+                        first = 64 * to_core + 32 * to_z
+                        ready[kk, to_core, to_z] = local[first:first + 32, :]
+                leave.pair(kk).start()
+                leave.start(0, kk)
                 if kk + 1 < BLOCKS:
                     after = at + BLOCK
                     turned_high, turned_low = split(mat[at:at + BLOCK, after:].T)
@@ -634,30 +744,12 @@
                                     mat[after:, part:part + BLOCK] = mat[after:, part:part + BLOCK] - piece
                         else:
                             mat[after:, start:start + 256] = mat[after:, start:start + 256] - change
+                leave.start(1, kk)
 
         return carry
 
     lax.fori_loop(0, BLOCKS, step, 0)
-    for i in range(BLOCKS):
-        at = i * BLOCK
-        inverse[at:at + BLOCK, :at + BLOCK] = mat[at:at + BLOCK, :at + BLOCK].astype(jnp.bfloat16)
-    for i in range(BLOCKS):
-        at = i * BLOCK
-        out[at:at + BLOCK, :] = dot(
-            inverse[at:at + BLOCK, :at + BLOCK], products[:at + BLOCK, :]
-        ).astype(jnp.bfloat16)
-
-
-def solve(gram, products):
-    return pl.pallas_call(
-        solve_kernel,
-        out_shape=jax.ShapeDtypeStruct(products.shape, jnp.bfloat16),
-        in_specs=[pl.BlockSpec(memory_space=pltpu.VMEM)] * 2,
-        out_specs=pl.BlockSpec(memory_space=pltpu.VMEM),
-        scratch_shapes=[pltpu.VMEM((NB, NB), jnp.float32), pltpu.VMEM((NB, NB), jnp.bfloat16)],
-        compiler_params=pltpu.CompilerParams(vmem_limit_bytes=VMEM),
-        name="factor_and_localize",
-    )(gram, products)
+    leave.finish()
 
 
 def pick(orbitals, pivots):
@@ -681,9 +773,8 @@
         )
         * (1.0 / math.sqrt(NB))
     ).astype(jnp.bfloat16)
-    gram = sum_gram(products)
-    local = solve(gram, products)
-    returned = give_back(local.reshape(entries))
+    landed = localize(products)
+    returned = give_back(landed.reshape(Z, CORES, Y, X, 2, points))
     return returned.reshape(512, 2, points).transpose(1, 0, 2).reshape(orbitals.shape)
 
 

time: 210 us -> 194 us (0.924)
  the two profiles are of different devices: /device:TPU:2 before, /device:TPU:1 now
where the time goes in v2:
time: 194 us
  Pallas kernels  182 us (94%)
  local copies, waits for them, and re-layouts  5.95 us (3%)
  matrix products  4.31 us (2%)
    pallas_call x1, Pallas kernels, localize(): pl.pallas_call(gram_kernel, out_shape=jax.ShapeDtypeStruct((Z, CORES, Y *...  121 us
    pallas_call x1, Pallas kernels, gather(): pl.pallas_call(gather_kernel, out_shape=[jax.ShapeDtypeStruct((Z, Y, CORE...  48.9 us
    pallas_call x1, Pallas kernels, give_back(): pl.pallas_call(return_kernel, out_shape=jax.ShapeDtypeStruct((Z, Y, CORES...  12.3 us

profile of v2, /device:TPU:1, one launch (start us, length us, event | category | flops | bytes accessed | tf_op | source)
XLA Modules:
  0.0 193.5 jit_solution(12566429755044517382)
XLA Ops:
  0.0 0.7 add_select_fusion
  0.7 0.0 copy-start
  0.7 0.1 iota_compare_fusion.2
  0.8 1.2 copy.8
  1.9 0.2 copy.4
  2.2 1.2 select_reduce_fusion
  3.3 0.0 copy-done
  3.4 48.9 %gather_slab_and_pivot_rows.1 = (bf16[16,4,2,4,2,256]{5,4,3,2,1,0:T(2,128)(2,1)S(1)}, bf16[16,4,2,4,16,128]{5,4,3,2,1,0:T(8,128)(2,1)S(1)}) custom-call(bf16[16,4,2,4,2,256]{5,4,3,2,1,0:T(2,128)(2,1)S(1)} %bitcast.30, bf16[16,128]{1,0:T(8,128)(2,1)S(1)} %convert_element_type.16.piece), custom_call_target="tpu_custom_call" | custom-call | tf_op jit(solution)/shard_map/gather_slab_and_pivot_rows/pallas_call | solution.py:272
  52.2 2.3 %reshape.73 = bf16[1024,1024]{1,0:T(8,128)(2,1)} reshape(bf16[16,4,2,4,16,128]{5,4,3,2,1,0:T(8,128)(2,1)S(1)} %get-tuple-element.7) | data formatting | bytes 4194304 | tf_op jit(solution)/shard_map/reshape | solution.py:771
  54.6 0.2 reshape.74
  54.8 3.1 %fusion.2.products = bf16[1024,256]{1,0:T(8,128)(2,1)} fusion(bf16[1024,1024]{1,0:T(8,128)(2,1)} %reshape.73, bf16[1024,256]{1,0:T(8,128)(2,1)S(1)} %reshape.74), kind=kOutput, calls=%fused_computation.4 | convolution fusion | flops 537395200 | bytes 3145728 | tf_op jit(solution)/shard_map/dot_general | solution.py:770
  57.9 121.2 %sum_factor_and_localize.1 = bf16[16,2,32,256]{3,2,1,0:T(8,128)(2,1)} custom-call(bf16[1024,256]{1,0:T(8,128)(2,1)} %fusion.2.products), custom_call_target="tpu_custom_call" | custom-call | tf_op jit(solution)/shard_map/sum_factor_and_localize/pallas_call | solution.py:503
  179.1 1.2 reshape.75.landed
  180.4 12.3 %return_localized.1 = bf16[16,4,2,4,2,256]{5,4,3,2,1,0:T(2,128)(2,1)S(1)} custom-call(bf16[16,2,4,4,2,256]{5,4,3,2,1,0:T(2,128)(2,1)S(1)} %reshape.75.landed), custom_call_target="tpu_custom_call" | custom-call | tf_op jit(solution)/shard_map/return_localized/pallas_call | solution.py:324
  192.7 0.8 copy.10
  (1 shorter events, 0.0 us)
Async XLA Ops:
  0.7 2.6 %copy-start = (bf16[2,131072]{1,0:T(2,128)(2,1)S(1)}, bf16[2,131072]{1,0:T(2,128)(2,1)}, u32[]{:S(2)}) copy-start(bf16[2,131072]{1,0:T(2,128)(2,1)} %param.2) | copy-start | bytes 1572868

commit v3 on v2

--- a/solution.py
+++ b/solution.py
@@ -16,7 +16,7 @@
 TILES = 576
 OWNERS = 9
 ROWS_OF_CORE = ((0, 3, 4, 7), (1, 2, 5, 6))
-VMEM = 56 * 1024 * 1024
+VMEM = 48 * 1024 * 1024
 
 
 def place():
@@ -187,25 +187,9 @@
             copy.wait_send()
 
 
-def regroup_scratch(points):
-    return [
-        pltpu.VMEM((Z, Y, X, 2, points), jnp.bfloat16),
-        pltpu.VMEM((CORES, Z, Y, X, 2, points), jnp.bfloat16),
-        pltpu.SemaphoreType.DMA,
-        pltpu.SemaphoreType.DMA,
-        pltpu.SemaphoreType.DMA((2, Z)),
-        pltpu.SemaphoreType.DMA((2, Z)),
-        pltpu.SemaphoreType.DMA((2, X * Y)),
-        pltpu.SemaphoreType.DMA((2, X * Y)),
-        pltpu.SemaphoreType.DMA((4,)),
-    ]
-
-
-def gather_kernel(orbitals, piece, slab, rows, beside, landed, *sems):
-    moving, sems = sems[:7], sems[7:]
+def gather_part(orbitals, piece, slab, rows, across, beside, landed, moving, sems, spot):
     q_send, q_recv, send, recv = sems
-    x, y, z, core = place()
-    greet(x, y, z, core, True)
+    x, y, z, core = spot
     regroup = Regroup(orbitals, slab, beside, landed, moving, (x, y, z, core))
     regroup.pair.start()
     first = []
@@ -259,105 +243,87 @@
     for copy in far:
         copy.wait_recv()
     forward(3, rows.at[:, :, core, lax.rem(x + 2, X)])
+    for copy in last:
+        copy.wait_recv()
+    for part in range(BLOCKS):
+        block = rows[2 * part:2 * part + 2].reshape(64, 16, 128).reshape(128, 8, 128).reshape(128, NB)
+        across[:, part * BLOCK:(part + 1) * BLOCK] = block.T
     regroup.start_plane(1)
-    for copy in last:
-        copy.wait_recv()
     regroup.finish()
     for copy in first + second + near + far + last:
         copy.wait_send()
 
 
-def gather(orbitals, piece):
-    points = orbitals.shape[-1]
-    return pl.pallas_call(
-        gather_kernel,
-        out_shape=[
-            jax.ShapeDtypeStruct((Z, Y, CORES, X, 2, points), jnp.bfloat16),
-            jax.ShapeDtypeStruct((Z, Y, CORES, X, 16, 128), jnp.bfloat16),
-        ],
-        in_specs=[pl.BlockSpec(memory_space=pltpu.VMEM)] * 2,
-        out_specs=[pl.BlockSpec(memory_space=pltpu.VMEM)] * 2,
-        scratch_shapes=regroup_scratch(points) + [
-            pltpu.SemaphoreType.DMA((Z,)),
-            pltpu.SemaphoreType.DMA((Z,)),
-            pltpu.SemaphoreType.DMA((3, 4)),
-            pltpu.SemaphoreType.DMA((3, 4)),
-        ],
-        compiler_params=pltpu.CompilerParams(
-            collective_id=0, has_side_effects=True, vmem_limit_bytes=32 * 1024 * 1024
-        ),
-        name="gather_slab_and_pivot_rows",
-    )(orbitals, piece)
-
-
-def return_kernel(landed, out, send, recv, kept):
-    x, y, z, core = place()
-    barrier = pltpu.get_barrier_semaphore()
-    partners = []
-    for along_y in range(Y):
-        for along_x in range(X):
-            if along_x or along_y:
-                partners.append((lax.rem(x + along_x, X), lax.rem(y + along_y, Y), along_y * X + along_x))
-    for to_x, to_y, _ in partners:
-        pl.semaphore_signal(barrier, inc=1, device_id=device(to_x, to_y, z, core), device_id_type=MESH)
-    pl.semaphore_wait(barrier, len(partners))
-    landing = out.at[:, y, :, x]
+def plane_part(landed, ordered, out, arrive, sems, spot):
+    send, recv, kept = sems
+    x, y, z, core = spot
     copies = []
-    for to_x, to_y, index in partners:
-        copy = remote(
-            landed.at[:, :, to_y, to_x], landing, send.at[index], recv.at[index], device(to_x, to_y, z, core)
-        )
-        copy.start()
-        copies.append(copy)
-    keep = pltpu.make_async_copy(landed.at[:, :, y, x], landing, kept)
-    keep.start()
-    keep.wait()
+    keeps = []
+    for turn, offset in enumerate((0, 1, 3, 2)):
+        first = lax.rem(z // 4 + offset, 4) * 4
+        for step in range(4):
+            arrive(first + step)
+        group = pl.ds(first, 4)
+        ordered[group] = landed[group].reshape(4, CORES, Y, X, 2, landed.shape[-1])
+        landing = out.at[group, y, :, x]
+        for along_y in range(Y):
+            for along_x in range(X):
+                if along_x or along_y:
+                    to_x, to_y = lax.rem(x + along_x, X), lax.rem(y + along_y, Y)
+                    index = along_y * X + along_x
+                    copy = remote(
+                        ordered.at[group, :, to_y, to_x], landing, send.at[turn, index], recv.at[turn, index],
+                        device(to_x, to_y, z, core),
+                    )
+                    copy.start()
+                    copies.append(copy)
+        keep = pltpu.make_async_copy(ordered.at[group, :, y, x], landing, kept.at[turn])
+        keep.start()
+        keeps.append(keep)
     for copy in copies:
         copy.wait_recv()
     for copy in copies:
         copy.wait_send()
-
-
-def give_back(landed):
-    points = landed.shape[-1]
-    dma = pltpu.SemaphoreType.DMA
-    return pl.pallas_call(
-        return_kernel,
-        out_shape=jax.ShapeDtypeStruct((Z, Y, CORES, X, 2, points), jnp.bfloat16),
-        in_specs=[pl.BlockSpec(memory_space=pltpu.VMEM)],
-        out_specs=pl.BlockSpec(memory_space=pltpu.VMEM),
-        scratch_shapes=[dma((X * Y,)), dma((X * Y,)), dma],
-        compiler_params=pltpu.CompilerParams(
-            collective_id=2, has_side_effects=True, vmem_limit_bytes=16 * 1024 * 1024
-        ),
-        name="return_localized",
-    )(landed)
-
-
-def gram_kernel(products, landed, out, theirs, terms, got0, got1, got2, got3, mat, ready, beside, send, recv, r_send, r_recv, z_send, z_recv, g_send, g_recv, p_send, p_recv, *leave):
-    x, y, z, core = place()
-    greet(x, y, z, core, False)
-    pair = remote(products, theirs, p_send, p_recv, device(x, y, z, 1 - core))
-    pair.start()
-    pair.wait_recv()
+    for keep in keeps:
+        keep.wait()
+
+
+def gram_part(across, slab, products, out, theirs, terms, got0, got1, got2, got3, sems, spot):
+    send, recv, r_send, r_recv, z_send, z_recv, g_send, g_recv, p_send, p_recv = sems
+    x, y, z, core = spot
+    pairs = []
+    columns = slab[...].reshape(NB, slab.shape[-1])
+    for part in range(4):
+        rows = slice(part * 256, (part + 1) * 256)
+        products[rows, :] = (dot(across[rows, :], columns) * (1.0 / math.sqrt(NB))).astype(jnp.bfloat16)
+        pair = remote(
+            products.at[rows, :], theirs.at[rows, :], p_send.at[part], p_recv.at[part], device(x, y, z, 1 - core)
+        )
+        pair.start()
+        pairs.append(pair)
     contract = (((1,), (1,)), ((), ()))
 
-    for which in range(CORES):
-
-        @pl.when(core == which)
-        def _():
-            count = 0
-            for i in ROWS_OF_CORE[which]:
-                rows = slice(i * BLOCK, (i + 1) * BLOCK)
-                rest = slice(i * BLOCK, NB)
-                row = lax.dot_general(
-                    products[rows, :], products[rest, :], contract, preferred_element_type=jnp.float32
-                ) + lax.dot_general(
-                    theirs[rows, :], theirs[rest, :], contract, preferred_element_type=jnp.float32
-                )
-                for j in range(BLOCKS - i):
-                    terms[count * 16:(count + 1) * 16] = row[:, j * BLOCK:(j + 1) * BLOCK].reshape(16, 8, 128)
-                    count += 1
+    def add(source, again):
+        for which in range(CORES):
+
+            @pl.when(core == which)
+            def _():
+                count = 0
+                for i in ROWS_OF_CORE[which]:
+                    row = lax.dot_general(
+                        source[i * BLOCK:(i + 1) * BLOCK, :], source[i * BLOCK:, :], contract,
+                        preferred_element_type=jnp.float32,
+                    )
+                    for j in range(BLOCKS - i):
+                        tiles = slice(count * 16, (count + 1) * 16)
+                        term = row[:, j * BLOCK:(j + 1) * BLOCK].reshape(16, 8, 128)
+                        terms[tiles] = terms[tiles] + term if again else term
+                        count += 1
+
+    add(products, False)
+    for pair in pairs:
+        pair.wait_recv()
+    add(theirs, True)
 
     unit = OWNERS
     half = 16 * unit
@@ -490,51 +456,8 @@
             for h in range(2):
                 to_all(step, h).wait_send()
 
-    for copy in copies + later:
+    for copy in copies + later + pairs:
         copy.wait_send()
-    pair.wait_send()
-    solve(out, products, landed, mat, ready, beside, leave, (x, y, z, core))
-
-
-def localize(products):
-    unit = OWNERS
-    points = products.shape[1]
-    dma = pltpu.SemaphoreType.DMA
-    return pl.pallas_call(
-        gram_kernel,
-        out_shape=jax.ShapeDtypeStruct((Z, CORES, Y * X * 2, points), jnp.bfloat16),
-        in_specs=[pl.BlockSpec(memory_space=pltpu.VMEM)],
-        out_specs=pl.BlockSpec(memory_space=pltpu.VMEM),
-        scratch_shapes=[
-            pltpu.VMEM((TILES, 8, 128), jnp.float32),
-            pltpu.VMEM(products.shape, jnp.bfloat16),
-            pltpu.VMEM((TILES // 2, 8, 128), jnp.float32),
-            pltpu.VMEM((2, 2, 2 * unit, 8, 128), jnp.float32),
-            pltpu.VMEM((2, 2, 4 * unit, 8, 128), jnp.float32),
-            pltpu.VMEM((2, 3, unit, 8, 128), jnp.float32),
-            pltpu.VMEM((Z - 1, 2, 8, 128), jnp.float32),
-            pltpu.VMEM((NB, NB), jnp.float32),
-            pltpu.VMEM((BLOCKS, CORES, 2, Y * X * 2, points), jnp.bfloat16),
-            pltpu.VMEM((BLOCKS, 2, Y * X * 2, points), jnp.bfloat16),
-            dma((3, 2, 4)),
-            dma((3, 2, 4)),
-            dma((3, 2, 4)),
-            dma((3, 2, 4)),
-            dma((Z, 2)),
-            dma((Z, 2)),
-            dma((Z, 2)),
-            dma((Z, 2)),
-            dma,
-            dma,
-            dma((BLOCKS,)),
-            dma((BLOCKS,)),
-            dma((2, Z)),
-            dma((2, Z)),
-            dma((2,)),
-        ],
-        compiler_params=pltpu.CompilerParams(collective_id=1, has_side_effects=True, vmem_limit_bytes=VMEM),
-        name="sum_factor_and_localize",
-    )(products)
 
 
 def split(value):
@@ -653,15 +576,24 @@
             def _():
                 self.keep(path, k, part).start()
 
-    def finish(self):
-        for path in range(2):
-            for step in range(1, Z):
-                source = lax.rem(self.z + step, Z)
+    def arrive(self, source):
+        @pl.when(self.z != source)
+        def _():
+            for path in range(2):
                 spot = self.landed.at[source, self.origin(path)]
                 remote(
                     spot, spot, self.z_send.at[path, source], self.z_recv.at[path, source],
                     device(self.x, self.y, source, self.core),
                 ).wait_recv()
+
+        @pl.when(self.z == source)
+        def _():
+            for path in range(2):
+                spot = self.landed.at[source, self.origin(path)]
+                pltpu.make_async_copy(spot, spot, self.local.at[path]).wait()
+
+    def finish(self):
+        for path in range(2):
             for k in range(BLOCKS):
                 for part in range(2):
 
@@ -669,15 +601,12 @@
                     def _():
                         self.along(path, k, part).wait_send()
 
-                    @pl.when(self.z == 2 * k + part)
-                    def _():
-                        self.keep(path, k, part).wait()
         for k in range(BLOCKS):
             self.pair(k).wait_send()
 
 
-def solve(gram, products, landed, mat, ready, beside, sems, spot):
-    leave = Leave(ready, beside, landed, sems, spot)
+def solve(gram, products, mat, leave):
+    ready = leave.ready
     lane = lax.broadcasted_iota(jnp.int32, (8, 128), 1)
     row = lax.broadcasted_iota(jnp.int32, (8, 128), 0)
     count = 0
@@ -749,7 +678,71 @@
         return carry
 
     lax.fori_loop(0, BLOCKS, step, 0)
+
+
+def whole_kernel(orbitals, piece, out, *scratch):
+    buffers, sems = scratch[:BUFFERS], scratch[BUFFERS:]
+    (
+        beside, landed, slab, rows, across, products, gram, theirs, terms, got0, got1, got2, got3,
+        mat, ready, beside2, landed2, ordered,
+    ) = buffers
+    spot = place()
+    greet(*spot, True)
+    gather_part(orbitals, piece, slab, rows, across, beside, landed, sems[:7], sems[7:11], spot)
+    gram_part(across, slab, products, gram, theirs, terms, got0, got1, got2, got3, sems[11:21], spot)
+    leave = Leave(ready, beside2, landed2, sems[21:26], spot)
+    solve(gram, products, mat, leave)
+    plane_part(landed2, ordered, out, leave.arrive, sems[26:29], spot)
     leave.finish()
+
+
+BUFFERS = 18
+
+
+def whole(orbitals, piece):
+    points = orbitals.shape[-1]
+    unit = OWNERS
+    dma = pltpu.SemaphoreType.DMA
+    narrow, wide = jnp.bfloat16, jnp.float32
+    entries = (Z, Y, CORES, X, 2, points)
+    held = Y * X * 2
+    buffers = [
+        pltpu.VMEM((Z, Y, X, 2, points), narrow),
+        pltpu.VMEM((CORES, Z, Y, X, 2, points), narrow),
+        pltpu.VMEM(entries, narrow),
+        pltpu.VMEM((Z, Y, CORES, X, 16, 128), narrow),
+        pltpu.VMEM((NB, NB), narrow),
+        pltpu.VMEM((NB, points), narrow),
+        pltpu.VMEM((TILES, 8, 128), wide),
+        pltpu.VMEM((NB, points), narrow),
+        pltpu.VMEM((TILES // 2, 8, 128), wide),
+        pltpu.VMEM((2, 2, 2 * unit, 8, 128), wide),
+        pltpu.VMEM((2, 2, 4 * unit, 8, 128), wide),
+        pltpu.VMEM((2, 3, unit, 8, 128), wide),
+        pltpu.VMEM((Z - 1, 2, 8, 128), wide),
+        pltpu.VMEM((NB, NB), wide),
+        pltpu.VMEM((BLOCKS, CORES, 2, held, points), narrow),
+        pltpu.VMEM((BLOCKS, 2, held, points), narrow),
+        pltpu.VMEM((Z, CORES, held, points), narrow),
+        pltpu.VMEM((Z, CORES, Y, X, 2, points), narrow),
+    ]
+    sems = [
+        dma, dma, dma((2, Z)), dma((2, Z)), dma((2, X * Y)), dma((2, X * Y)), dma((4,)),
+        dma((Z,)), dma((Z,)), dma((3, 4)), dma((3, 4)),
+        dma((3, 2, 4)), dma((3, 2, 4)), dma((3, 2, 4)), dma((3, 2, 4)),
+        dma((Z, 2)), dma((Z, 2)), dma((Z, 2)), dma((Z, 2)), dma((4,)), dma((4,)),
+        dma((BLOCKS,)), dma((BLOCKS,)), dma((2, Z)), dma((2, Z)), dma((2,)),
+        dma((4, X * Y)), dma((4, X * Y)), dma((4,)),
+    ]
+    return pl.pallas_call(
+        whole_kernel,
+        out_shape=jax.ShapeDtypeStruct(entries, narrow),
+        in_specs=[pl.BlockSpec(memory_space=pltpu.VMEM)] * 2,
+        out_specs=pl.BlockSpec(memory_space=pltpu.VMEM),
+        scratch_shapes=buffers + sems,
+        compiler_params=pltpu.CompilerParams(collective_id=0, has_side_effects=True, vmem_limit_bytes=VMEM),
+        name="localize",
+    )(orbitals, piece)
 
 
 def pick(orbitals, pivots):
@@ -765,16 +758,7 @@
     entries = (Z, Y, CORES, X, 2, points)
     piece = pick(orbitals, pivots).reshape(16, 128)
     outgoing = orbitals.reshape(2, 512, points).transpose(1, 0, 2).reshape(entries)
-    slab, rows = gather(outgoing, piece)
-    products = (
-        lax.dot_general(
-            rows.reshape(NB, NB), slab.reshape(NB, points), (((0,), (0,)), ((), ())),
-            preferred_element_type=jnp.float32,
-        )
-        * (1.0 / math.sqrt(NB))
-    ).astype(jnp.bfloat16)
-    landed = localize(products)
-    returned = give_back(landed.reshape(Z, CORES, Y, X, 2, points))
+    returned = whole(outgoing, piece)
     return returned.reshape(512, 2, points).transpose(1, 0, 2).reshape(orbitals.shape)
 
 

time: 194 us -> 171 us (0.88)
  the two profiles are of different devices: /device:TPU:1 before, /device:TPU:480 now
where the time goes in v3:
time: 171 us
  Pallas kernels  167 us (98%)
  local copies, waits for them, and re-layouts  2.14 us (1%)
    pallas_call x1, Pallas kernels, whole(): pl.pallas_call(whole_kernel, out_shape=jax.ShapeDtypeStruct(entries, narr...  167 us

profile of v3, /device:TPU:480, one launch (start us, length us, event | category | flops | bytes accessed | tf_op | source)
XLA Modules:
  0.0 170.7 jit_solution(10787551268387424659)
XLA Ops:
  0.0 0.7 add_select_fusion
  0.7 0.1 iota_compare_fusion.2
  0.8 1.1 copy.8
  1.9 0.2 copy.4
  2.1 0.0 copy-start
  2.1 1.2 select_reduce_fusion
  3.3 0.0 copy-done
  3.3 166.6 %localize.1 = bf16[16,4,2,4,2,256]{5,4,3,2,1,0:T(2,128)(2,1)S(1)} custom-call(bf16[16,4,2,4,2,256]{5,4,3,2,1,0:T(2,128)(2,1)S(1)} %bitcast.24, bf16[16,128]{1,0:T(8,128)(2,1)S(1)} %convert_element_type.13.piece), custom_call_target="tpu_custom_call" | custom-call | tf_op jit(solution)/shard_map/localize/pallas_call | solution.py:737
  169.9 0.8 copy.10
  (1 shorter events, 0.0 us)
Async XLA Ops:
  2.1 1.2 copy-start

commit v4 on v3

--- a/solution.py
+++ b/solution.py
@@ -129,59 +129,74 @@
             device(self.x, self.y, self.z, 1 - self.core),
         )
         self.done = []
-        self.paths = []
         self.plane = []
+        self.kept = []
 
     def leaving(self, path, z):
         return self.source.at[z, :, self.core] if path == 0 else self.beside.at[z]
+
+    def landing(self, path, z):
+        return self.landed.at[self.origin[path], z]
 
     def start_z(self, path):
         x, y, z, core = self.x, self.y, self.z, self.core
         if path == 1:
             self.pair.wait_recv()
-        landing = self.landed.at[self.origin[path], z]
-        copies = []
         for step in order_of_z():
             target = lax.rem(z + step, Z)
             copy = remote(
-                self.leaving(path, target), landing, self.z_send.at[path, step], self.z_recv.at[path, step],
+                self.leaving(path, target), self.landing(path, z), self.z_send.at[path, step], self.z_recv.at[path, z],
                 device(x, y, target, core),
             )
             copy.start()
-            copies.append(copy)
-        own = pltpu.make_async_copy(self.leaving(path, z), landing, self.local.at[path])
-        own.start()
-        self.paths.append((own, copies))
+            self.done.append(copy)
+        pltpu.make_async_copy(self.leaving(path, z), self.landing(path, z), self.local.at[path]).start()
+
+    def arrive(self, path, source):
+        spot = self.landing(path, source)
+
+        @pl.when(self.z != source)
+        def _():
+            remote(
+                spot, spot, self.z_send.at[path, 0], self.z_recv.at[path, source],
+                device(self.x, self.y, source, self.core),
+            ).wait_recv()
+
+        @pl.when(self.z == source)
+        def _():
+            pltpu.make_async_copy(spot, spot, self.local.at[path]).wait()
 
     def start_plane(self, path):
         x, y, z, core = self.x, self.y, self.z, self.core
-        own, copies = self.paths[path]
-        own.wait()
-        for copy in copies:
-            copy.wait_recv()
-        self.done += copies
         origin = self.origin[path]
-        landing = self.out.at[:, y, origin, x]
-        for along_y in range(Y):
-            for along_x in range(X):
-                if along_x or along_y:
-                    to_x, to_y = lax.rem(x + along_x, X), lax.rem(y + along_y, Y)
-                    index = along_y * X + along_x
-                    copy = remote(
-                        self.landed.at[origin, :, to_y, to_x], landing,
-                        self.y_send.at[path, index], self.y_recv.at[path, index],
-                        device(to_x, to_y, z, core),
-                    )
-                    copy.start()
-                    self.plane.append(copy)
-        keep = pltpu.make_async_copy(self.landed.at[origin, :, y, x], landing, self.local.at[2 + path])
-        keep.start()
-        self.done_keep = getattr(self, "done_keep", []) + [keep]
+        for turn, offset in enumerate((0, 1, 3, 2)):
+            first = lax.rem(z // 4 + offset, 4) * 4
+            for step in range(4):
+                self.arrive(path, first + step)
+            group = pl.ds(first, 4)
+            landing = self.out.at[group, y, origin, x]
+            for along_y in range(Y):
+                for along_x in range(X):
+                    if along_x or along_y:
+                        to_x, to_y = lax.rem(x + along_x, X), lax.rem(y + along_y, Y)
+                        index = along_y * X + along_x
+                        copy = remote(
+                            self.landed.at[origin, group, to_y, to_x], landing,
+                            self.y_send.at[path, turn, index], self.y_recv.at[path, turn, index],
+                            device(to_x, to_y, z, core),
+                        )
+                        copy.start()
+                        self.plane.append(copy)
+            keep = pltpu.make_async_copy(
+                self.landed.at[origin, group, y, x], landing, self.local.at[2 + 4 * path + turn]
+            )
+            keep.start()
+            self.kept.append(keep)
 
     def finish(self):
         for copy in self.plane:
             copy.wait_recv()
-        for keep in self.done_keep:
+        for keep in self.kept:
             keep.wait()
         for copy in self.plane + self.done + [self.pair]:
             copy.wait_send()
@@ -288,7 +303,7 @@
         keep.wait()
 
 
-def gram_part(across, slab, products, out, theirs, terms, got0, got1, got2, got3, sems, spot):
+def gram_part(across, slab, products, out, theirs, terms, got0, got1, got2, got3, plane, summed, sems, spot):
     send, recv, r_send, r_recv, z_send, z_recv, g_send, g_recv, p_send, p_recv = sems
     x, y, z, core = spot
     pairs = []
@@ -385,76 +400,63 @@
     starts = [h * half + (firsts[h] * 4 + seconds[h]) * unit for h in range(2)]
     for h in range(2):
         mine = pl.ds(starts[h], unit)
-        terms[mine] = terms[mine] + (got2[h, 0] + got2[h, 1]) + got2[h, 2]
-
-    def to_owner(step, h):
+        plane[:, h] = terms[mine] + (got2[h, 0] + got2[h, 1]) + got2[h, 2]
+
+    def to_owner(step):
         target = lax.rem(z + step, Z)
         tile = jnp.minimum(target, OWNERS - 1)
         return target, remote(
-            terms.at[starts[h] + tile],
-            got3.at[step - 1, h],
-            z_send.at[step, h],
-            z_recv.at[step, h],
-            device(x, y, target, core),
-        )
+            plane.at[tile], got3.at[step - 1], z_send.at[step], z_recv.at[step], device(x, y, target, core)
+        )
+
+    for step in order_of_z():
+        target, copy = to_owner(step)
+
+        @pl.when(target < OWNERS)
+        def _():
+            copy.start()
+
+    tile = jnp.minimum(z, OWNERS - 1)
+
+    def to_all(step):
+        return remote(
+            summed.at[tile], summed.at[tile], g_send.at[step], g_recv.at[step],
+            device(x, y, lax.rem(z + step, Z), core),
+        )
+
+    @pl.when(z < OWNERS)
+    def _():
+        for step in order_of_z():
+            to_owner(step)[1].wait_recv()
+        total = plane[tile]
+        for step in range(1, Z):
+            total = total + got3[step - 1]
+        summed[tile] = total
+        for step in order_of_z():
+            to_all(step).start()
+
+    for step in order_of_z():
+        source = lax.rem(z + Z - step, Z)
+
+        @pl.when(source < OWNERS)
+        def _():
+            to_all(step).wait_recv()
+
+    for h in range(2):
+        out[pl.ds(core * 2 * half + starts[h], unit)] = summed[:, h]
+    spread(out, unit, x, y, z, core, send, recv)
 
     for step in range(1, Z):
-        for h in range(2):
-            target, copy = to_owner(step, h)
-
-            @pl.when(target < OWNERS)
-            def _():
-                copy.start()
-
-    goals = [core * 2 * half + starts[h] for h in range(2)]
-    tile = jnp.minimum(z, OWNERS - 1)
-
-    def to_all(step, h):
-        return remote(
-            out.at[goals[h] + tile],
-            out.at[goals[h] + tile],
-            g_send.at[step, h],
-            g_recv.at[step, h],
-            device(x, y, lax.rem(z + step, Z), core),
-        )
+        target, copy = to_owner(step)
+
+        @pl.when(target < OWNERS)
+        def _():
+            copy.wait_send()
 
     @pl.when(z < OWNERS)
     def _():
         for step in range(1, Z):
-            for h in range(2):
-                to_owner(step, h)[1].wait_recv()
-        for h in range(2):
-            total = terms[starts[h] + tile]
-            for step in range(1, Z):
-                total = total + got3[step - 1, h]
-            out[goals[h] + tile] = total
-        for step in range(1, Z):
-            for h in range(2):
-                to_all(step, h).start()
-
-    for step in range(1, Z):
-        source = lax.rem(z + Z - step, Z)
-
-        @pl.when(source < OWNERS)
-        def _():
-            for h in range(2):
-                to_all(step, h).wait_recv()
-
-    spread(out, unit, x, y, z, core, send, recv)
-
-    for step in range(1, Z):
-        for h in range(2):
-            target, copy = to_owner(step, h)
-
-            @pl.when(target < OWNERS)
-            def _():
-                copy.wait_send()
-
-    @pl.when(z < OWNERS)
-    def _():
-        for step in range(1, Z):
-            for h in range(2):
-                to_all(step, h).wait_send()
+            to_all(step).wait_send()
 
     for copy in copies + later + pairs:
         copy.wait_send()
@@ -620,83 +622,76 @@
             if i:
                 mat[i * BLOCK:(i + 1) * BLOCK, :i * BLOCK] = jnp.zeros((BLOCK, i * BLOCK), jnp.float32)
 
-    def step(k, carry):
-        begin = pl.multiple_of(k * BLOCK, BLOCK)
-        own = pl.ds(begin, BLOCK)
-
-        def load(g):
-            return mat[pl.ds(pl.multiple_of(begin + 8 * g, 8), 8), own]
-
-        for g, value in enumerate(factor_block(load, lane, row)):
-            mat[pl.ds(pl.multiple_of(begin + 8 * g, 8), 8), own] = value
-        for kk in range(BLOCKS):
-
-            @pl.when(k == kk)
-            def _():
-                at = kk * BLOCK
-                high, low = split(mat[at:at + BLOCK, at:at + BLOCK])
-                left = jnp.concatenate([high, low], axis=1)
-                spans = [(0, at), (at + BLOCK, NB)]
-                for start, stop in spans:
-                    if start < stop:
-                        up, down = split(mat[at:at + BLOCK, start:stop])
-                        mat[at:at + BLOCK, start:stop] = dot(left, jnp.concatenate([up, up], axis=0)) + dot(high, down)
-                inverse = jnp.concatenate(
-                    [
-                        mat[at + 64 * to_z + 16 * to_y + 8 * to_core:at + 64 * to_z + 16 * to_y + 8 * to_core + 8, :at + BLOCK]
-                        for to_core in range(CORES)
-                        for to_z in range(2)
-                        for to_y in range(Y)
-                    ],
-                    axis=0,
-                ).astype(jnp.bfloat16)
-                local = dot(inverse, products[:at + BLOCK, :]).astype(jnp.bfloat16)
-                for to_core in range(CORES):
-                    for to_z in range(2):
-                        first = 64 * to_core + 32 * to_z
-                        ready[kk, to_core, to_z] = local[first:first + 32, :]
-                leave.pair(kk).start()
-                leave.start(0, kk)
-                if kk + 1 < BLOCKS:
-                    after = at + BLOCK
-                    turned_high, turned_low = split(mat[at:at + BLOCK, after:].T)
-                    turned = jnp.concatenate([turned_high, turned_low], axis=1)
-                    for start in range(0, NB, 256):
-                        up, down = split(mat[at:at + BLOCK, start:start + 256])
-                        change = dot(turned, jnp.concatenate([up, up], axis=0)) + dot(turned_high, down)
-                        if start <= at < start + 256:
-                            for part in (start, start + BLOCK):
-                                piece = change[:, part - start:part - start + BLOCK]
-                                if part == at:
-                                    mat[after:, part:part + BLOCK] = -piece
-                                else:
-                                    mat[after:, part:part + BLOCK] = mat[after:, part:part + BLOCK] - piece
-                        else:
-                            mat[after:, start:start + 256] = mat[after:, start:start + 256] - change
-                leave.start(1, kk)
-
-        return carry
-
-    lax.fori_loop(0, BLOCKS, step, 0)
+    first = mat[:BLOCK, :BLOCK]
+    own = jnp.concatenate(factor_block(lambda g: first[8 * g:8 * g + 8, :], lane, row), axis=0)
+    for k in range(BLOCKS):
+        at = k * BLOCK
+        after = at + BLOCK
+        here = slice(at, after)
+        mat[here, here] = own
+        high, low = split(own)
+        left = jnp.concatenate([high, low], axis=1)
+        for start, stop in ((0, at), (after, NB)):
+            if start < stop:
+                up, down = split(mat[here, start:stop])
+                mat[here, start:stop] = dot(left, jnp.concatenate([up, up], axis=0)) + dot(high, down)
+        if after < NB:
+            turned_high, turned_low = split(mat[here, after:].T)
+            turned = jnp.concatenate([turned_high, turned_low], axis=1)
+
+            def change(begin, end, start, stop):
+                rows = slice(begin - after, end - after)
+                up, down = split(mat[here, start:stop])
+                return dot(turned[rows], jnp.concatenate([up, up], axis=0)) + dot(turned_high[rows], down)
+
+            following = slice(after, after + BLOCK)
+            corner = mat[following, following] - change(after, after + BLOCK, after, after + BLOCK)
+            own = jnp.concatenate(factor_block(lambda g: corner[8 * g:8 * g + 8, :], lane, row), axis=0)
+            mat[after:, here] = -change(after, NB, at, after)
+            for start in range(0, at, 256):
+                stop = min(start + 256, at)
+                mat[after:, start:stop] = mat[after:, start:stop] - change(after, NB, start, stop)
+            for start in range(after, NB, 256):
+                stop = min(start + 256, NB)
+                mat[after:stop, start:stop] = mat[after:stop, start:stop] - change(after, stop, start, stop)
+        inverse = jnp.concatenate(
+            [
+                mat[at + 64 * to_z + 16 * to_y + 8 * to_core:at + 64 * to_z + 16 * to_y + 8 * to_core + 8, :after]
+                for to_core in range(CORES)
+                for to_z in range(2)
+                for to_y in range(Y)
+            ],
+            axis=0,
+        ).astype(jnp.bfloat16)
+        local = dot(inverse, products[:after, :]).astype(jnp.bfloat16)
+        for to_core in range(CORES):
+            for to_z in range(2):
+                begin = 64 * to_core + 32 * to_z
+                ready[k, to_core, to_z] = local[begin:begin + 32, :]
+        leave.pair(k).start()
+        leave.start(0, k)
+        if k:
+            leave.start(1, k - 1)
+    leave.start(1, BLOCKS - 1)
 
 
 def whole_kernel(orbitals, piece, out, *scratch):
     buffers, sems = scratch[:BUFFERS], scratch[BUFFERS:]
     (
         beside, landed, slab, rows, across, products, gram, theirs, terms, got0, got1, got2, got3,
-        mat, ready, beside2, landed2, ordered,
+        plane, summed, mat, ready, beside2, landed2, ordered,
     ) = buffers
     spot = place()
     greet(*spot, True)
     gather_part(orbitals, piece, slab, rows, across, beside, landed, sems[:7], sems[7:11], spot)
-    gram_part(across, slab, products, gram, theirs, terms, got0, got1, got2, got3, sems[11:21], spot)
+    gram_part(across, slab, products, gram, theirs, terms, got0, got1, got2, got3, plane, summed, sems[11:21], spot)
     leave = Leave(ready, beside2, landed2, sems[21:26], spot)
     solve(gram, products, mat, leave)
     plane_part(landed2, ordered, out, leave.arrive, sems[26:29], spot)
     leave.finish()
 
 
-BUFFERS = 18
+BUFFERS = 20
 
 
 def whole(orbitals, piece):
@@ -720,6 +715,8 @@
         pltpu.VMEM((2, 2, 4 * unit, 8, 128), wide),
         pltpu.VMEM((2, 3, unit, 8, 128), wide),
         pltpu.VMEM((Z - 1, 2, 8, 128), wide),
+        pltpu.VMEM((OWNERS, 2, 8, 128), wide),
+        pltpu.VMEM((OWNERS, 2, 8, 128), wide),
         pltpu.VMEM((NB, NB), wide),
         pltpu.VMEM((BLOCKS, CORES, 2, held, points), narrow),
         pltpu.VMEM((BLOCKS, 2, held, points), narrow),
@@ -727,10 +724,10 @@
         pltpu.VMEM((Z, CORES, Y, X, 2, points), narrow),
     ]
     sems = [
-        dma, dma, dma((2, Z)), dma((2, Z)), dma((2, X * Y)), dma((2, X * Y)), dma((4,)),
+        dma, dma, dma((2, Z)), dma((2, Z)), dma((2, 4, X * Y)), dma((2, 4, X * Y)), dma((10,)),
         dma((Z,)), dma((Z,)), dma((3, 4)), dma((3, 4)),
         dma((3, 2, 4)), dma((3, 2, 4)), dma((3, 2, 4)), dma((3, 2, 4)),
-        dma((Z, 2)), dma((Z, 2)), dma((Z, 2)), dma((Z, 2)), dma((4,)), dma((4,)),
+        dma((Z,)), dma((Z,)), dma((Z,)), dma((Z,)), dma((4,)), dma((4,)),
         dma((BLOCKS,)), dma((BLOCKS,)), dma((2, Z)), dma((2, Z)), dma((2,)),
         dma((4, X * Y)), dma((4, X * Y)), dma((4,)),
     ]

time: 171 us -> 171 us (level)
  no operation moved by 1% of the time
where the time goes in v4:
time: 171 us
  Pallas kernels  167 us (98%)
  local copies, waits for them, and re-layouts  2.14 us (1%)
    pallas_call x1, Pallas kernels, whole(): pl.pallas_call(whole_kernel, out_shape=jax.ShapeDtypeStruct(entries, narr...  167 us

profile of v4, /device:TPU:480, one launch (start us, length us, event | category | flops | bytes accessed | tf_op | source)
XLA Modules:
  0.0 171.2 jit_solution(14075163300198556707)
XLA Ops:
  0.0 0.7 add_select_fusion
  0.7 0.1 iota_compare_fusion.2
  0.8 1.1 copy.8
  1.9 0.2 copy.4
  2.1 0.0 copy-start
  2.1 1.2 select_reduce_fusion
  3.3 0.0 copy-done
  3.3 167.1 %localize.1 = bf16[16,4,2,4,2,256]{5,4,3,2,1,0:T(2,128)(2,1)S(1)} custom-call(bf16[16,4,2,4,2,256]{5,4,3,2,1,0:T(2,128)(2,1)S(1)} %bitcast.24, bf16[16,128]{1,0:T(8,128)(2,1)S(1)} %convert_element_type.13.piece), custom_call_target="tpu_custom_call" | custom-call | tf_op jit(solution)/shard_map/localize/pallas_call | solution.py:734
  170.4 0.8 copy.10
  (1 shorter events, 0.0 us)
Async XLA Ops:
  2.1 1.2 copy-start

commit v5 on v4

--- a/solution.py
+++ b/solution.py
@@ -14,7 +14,8 @@
 BLOCK = 128
 BLOCKS = NB // BLOCK
 TILES = 576
-OWNERS = 9
+UNITS = (5, 4)
+OWNERS = (0, 8)
 ROWS_OF_CORE = ((0, 3, 4, 7), (1, 2, 5, 6))
 VMEM = 48 * 1024 * 1024
 
@@ -46,67 +47,6 @@
     return pltpu.make_async_remote_copy(
         src_ref=src, dst_ref=dst, send_sem=send, recv_sem=recv, device_id=target, device_id_type=MESH
     )
-
-
-def spread(out, unit, x, y, z, core, send, recv):
-    half = 16 * unit
-    base = core * 2 * half
-    firsts = (x, y)
-    seconds = (y, x)
-
-    def mate(axis_is_x, step):
-        if axis_is_x:
-            return device(lax.rem(x + step, X), y, z, core)
-        return device(x, lax.rem(y + step, Y), z, core)
-
-    started = []
-    inner = []
-    for h in range(2):
-        mine = out.at[pl.ds(base + h * half + (firsts[h] * 4 + seconds[h]) * unit, unit)]
-        for step in range(1, 4):
-            copy = remote(mine, mine, send.at[0, h, step], recv.at[0, h, step], mate(h == 1, step))
-            copy.start()
-            inner.append(copy)
-    for copy in inner:
-        copy.wait_recv()
-    started += inner
-    sibling = device(x, y, z, 1 - core)
-    across = []
-    near = []
-    block = 4 * unit
-
-    def part(h, where, begin=0, size=block):
-        return out.at[pl.ds(base + h * half + lax.rem(firsts[h] + where, 4) * block + begin, size)]
-
-    def forward(h, index, ref):
-        copy = remote(ref, ref, send.at[2, h, index], recv.at[2, h, index], sibling)
-        copy.start()
-        across.append(copy)
-
-    for h in range(2):
-        for index, step in ((0, 1), (1, 3)):
-            copy = remote(part(h, 0), part(h, 0), send.at[1, h, index], recv.at[1, h, index], mate(h == 0, step))
-            copy.start()
-            near.append((h, index, step, copy))
-    for h in range(2):
-        forward(h, 0, part(h, 0))
-    far = []
-    for h, index, step, copy in near:
-        copy.wait_recv()
-        ref = part(h, 4 - step, index * (block // 2), block // 2)
-        onward = remote(ref, ref, send.at[1, h, 2 + index], recv.at[1, h, 2 + index], mate(h == 0, step))
-        onward.start()
-        far.append(onward)
-        forward(h, 1 + index, part(h, 4 - step))
-        started.append(copy)
-    for copy in far:
-        copy.wait_recv()
-    for h in range(2):
-        forward(h, 3, part(h, 2))
-    for copy in across:
-        copy.wait_recv()
-    for copy in started + far + across:
-        copy.wait_send()
 
 
 def order_of_z():
@@ -303,8 +243,184 @@
         keep.wait()
 
 
-def gram_part(across, slab, products, out, theirs, terms, got0, got1, got2, got3, plane, summed, sems, spot):
-    send, recv, r_send, r_recv, z_send, z_recv, g_send, g_recv, p_send, p_recv = sems
+def sum_wave(wave, out, terms, buffers, sems, spot):
+    got0, got1, got2, got3, plane, summed = buffers
+    send, recv, r_send, r_recv, z_send, z_recv, g_send, g_recv = sems
+    x, y, z, core = spot
+    unit = UNITS[wave]
+    first_owner = OWNERS[wave]
+    half = 16 * unit
+    block = 4 * unit
+    middle = block // 2
+    begin = sum(UNITS[:wave]) * 32
+    goal = core * (TILES // 2) + begin
+    firsts = (x, y)
+    seconds = (y, x)
+    sent = []
+
+    def mate(axis_is_x, step):
+        if axis_is_x:
+            return device(lax.rem(x + step, X), y, z, core)
+        return device(x, lax.rem(y + step, Y), z, core)
+
+    def span(base, h, where, start=0, size=block):
+        return pl.ds(base + h * half + lax.rem(firsts[h] + where, 4) * block + start, size)
+
+    def launch(*args):
+        copy = remote(*args)
+        copy.start()
+        sent.append(copy)
+        return copy
+
+    far = [
+        (h, index, step, launch(
+            terms.at[span(begin, h, 2, index * middle, middle)], got0.at[h, index],
+            r_send.at[wave, 0, h, index], r_recv.at[wave, 0, h, index], mate(h == 0, step),
+        ))
+        for h in range(2) for index, step in ((0, 1), (1, 3))
+    ]
+    yield
+    near = []
+    for h, index, step, copy in far:
+        copy.wait_recv()
+        part = span(begin, h, step, index * middle, middle)
+        terms[part] = terms[part] + got0[h, index]
+        near.append(launch(
+            terms.at[span(begin, h, step)], got1.at[h, index], r_send.at[wave, 2, h, index],
+            r_recv.at[wave, 2, h, index], mate(h == 0, step),
+        ))
+    yield
+    for copy in near:
+        copy.wait_recv()
+    later = []
+    for h in range(2):
+        mine = span(begin, h, 0)
+        terms[mine] = terms[mine] + (got1[h, 0] + got1[h, 1])
+    for step in range(1, 4):
+        for h in range(2):
+            target = lax.rem(seconds[h] + step, 4)
+            later.append(launch(
+                terms.at[pl.ds(begin + h * half + (firsts[h] * 4 + target) * unit, unit)], got2.at[h, step - 1],
+                r_send.at[wave, 1, h, step], r_recv.at[wave, 1, h, step], mate(h == 1, step),
+            ))
+    yield
+    for copy in later:
+        copy.wait_recv()
+    starts = [h * half + (firsts[h] * 4 + seconds[h]) * unit for h in range(2)]
+    for h in range(2):
+        mine = pl.ds(begin + starts[h], unit)
+        plane[:, h] = terms[mine] + (got2[h, 0] + got2[h, 1]) + got2[h, 2]
+
+    def owns(where):
+        return (where >= first_owner) & (where < first_owner + unit)
+
+    def tile_of(where):
+        return jnp.clip(where - first_owner, 0, unit - 1)
+
+    def to_owner(step):
+        target = lax.rem(z + step, Z)
+        return target, remote(
+            plane.at[tile_of(target)], got3.at[step - 1], z_send.at[wave, step], z_recv.at[wave, step],
+            device(x, y, target, core),
+        )
+
+    for step in order_of_z():
+        target, copy = to_owner(step)
+
+        @pl.when(owns(target))
+        def _():
+            copy.start()
+
+    yield
+    tile = tile_of(z)
+
+    def to_all(step, which):
+        return remote(
+            summed.at[which], summed.at[which], g_send.at[wave, step], g_recv.at[wave, step],
+            device(x, y, lax.rem(z + step, Z), core),
+        )
+
+    @pl.when(owns(z))
+    def _():
+        for step in order_of_z():
+            to_owner(step)[1].wait_recv()
+        total = plane[tile]
+        for step in range(1, Z):
+            total = total + got3[step - 1]
+        summed[tile] = total
+        for step in order_of_z():
+            to_all(step, tile).start()
+
+    yield
+    for step in order_of_z():
+        source = lax.rem(z + Z - step, Z)
+
+        @pl.when(owns(source))
+        def _():
+            to_all(step, tile_of(source)).wait_recv()
+
+    inner = []
+    for h in range(2):
+        own = pl.ds(goal + starts[h], unit)
+        out[own] = summed[:, h]
+        for step in range(1, 4):
+            inner.append(launch(
+                out.at[own], out.at[own], send.at[wave, 0, h, step], recv.at[wave, 0, h, step], mate(h == 1, step)
+            ))
+    yield
+    for copy in inner:
+        copy.wait_recv()
+    across = []
+
+    def forward(h, index, ref):
+        across.append(launch(
+            ref, ref, send.at[wave, 2, h, index], recv.at[wave, 2, h, index], device(x, y, z, 1 - core)
+        ))
+
+    near = []
+    for h in range(2):
+        ref = out.at[span(goal, h, 0)]
+        for index, step in ((0, 1), (1, 3)):
+            near.append((h, index, step, launch(
+                ref, ref, send.at[wave, 1, h, index], recv.at[wave, 1, h, index], mate(h == 0, step)
+            )))
+    for h in range(2):
+        forward(h, 0, out.at[span(goal, h, 0)])
+    yield
+    far = []
+    for h, index, step, copy in near:
+        copy.wait_recv()
+        ref = out.at[span(goal, h, 4 - step, index * middle, middle)]
+        far.append(launch(
+            ref, ref, send.at[wave, 1, h, 2 + index], recv.at[wave, 1, h, 2 + index], mate(h == 0, step)
+        ))
+        forward(h, 1 + index, out.at[span(goal, h, 4 - step)])
+    yield
+    for copy in far:
+        copy.wait_recv()
+    for h in range(2):
+        forward(h, 3, out.at[span(goal, h, 2)])
+    yield
+    for copy in across:
+        copy.wait_recv()
+    yield
+    for copy in sent:
+        copy.wait_send()
+    for step in range(1, Z):
+        target, copy = to_owner(step)
+
+        @pl.when(owns(target))
+        def _():
+            copy.wait_send()
+
+    @pl.when(owns(z))
+    def _():
+        for step in range(1, Z):
+            to_all(step, tile).wait_send()
+
+
+def gram_part(across, slab, products, out, theirs, terms, buffers, sems, spot):
+    p_send, p_recv = sems[-2:]
     x, y, z, core = spot
     pairs = []
     columns = slab[...].reshape(NB, slab.shape[-1])
@@ -318,13 +434,13 @@
         pairs.append(pair)
     contract = (((1,), (1,)), ((), ()))
 
-    def add(source, again):
+    def add(source, again, begin, end):
         for which in range(CORES):
 
             @pl.when(core == which)
             def _():
-                count = 0
-                for i in ROWS_OF_CORE[which]:
+                count = sum(BLOCKS - i for i in ROWS_OF_CORE[which][:begin])
+                for i in ROWS_OF_CORE[which][begin:end]:
                     row = lax.dot_general(
                         source[i * BLOCK:(i + 1) * BLOCK, :], source[i * BLOCK:, :], contract,
                         preferred_element_type=jnp.float32,
@@ -335,131 +451,18 @@
                         terms[tiles] = terms[tiles] + term if again else term
                         count += 1
 
-    add(products, False)
+    add(products, False, 0, 4)
     for pair in pairs:
         pair.wait_recv()
-    add(theirs, True)
-
-    unit = OWNERS
-    half = 16 * unit
-    firsts = (x, y)
-    seconds = (y, x)
-
-    def mate(axis_is_x, step):
-        if axis_is_x:
-            return device(lax.rem(x + step, X), y, z, core)
-        return device(x, lax.rem(y + step, Y), z, core)
-
-    block = 4 * unit
-    middle = block // 2
-
-    def span(h, where, begin=0, size=block):
-        return pl.ds(h * half + lax.rem(firsts[h] + where, 4) * block + begin, size)
-
-    copies = []
-    for h in range(2):
-        for index, step in ((0, 1), (1, 3)):
-            copy = remote(
-                terms.at[span(h, 2, index * middle, middle)], got0.at[h, index],
-                r_send.at[0, h, index], r_recv.at[0, h, index], mate(h == 0, step),
-            )
-            copy.start()
-            copies.append((h, index, step, copy))
-    near = []
-    for h, index, step, copy in copies:
-        copy.wait_recv()
-        part = span(h, step, index * middle, middle)
-        terms[part] = terms[part] + got0[h, index]
-        onward = remote(
-            terms.at[span(h, step)], got1.at[h, index], r_send.at[2, h, index], r_recv.at[2, h, index],
-            mate(h == 0, step),
-        )
-        onward.start()
-        near.append(onward)
-    copies = [copy for _, _, _, copy in copies] + near
-    for copy in near:
-        copy.wait_recv()
-    for h in range(2):
-        mine = span(h, 0)
-        terms[mine] = terms[mine] + (got1[h, 0] + got1[h, 1])
-    later = []
-    for step in range(1, 4):
-        for h in range(2):
-            target = lax.rem(seconds[h] + step, 4)
-            copy = remote(
-                terms.at[pl.ds(h * half + (firsts[h] * 4 + target) * unit, unit)],
-                got2.at[h, step - 1],
-                r_send.at[1, h, step],
-                r_recv.at[1, h, step],
-                mate(h == 1, step),
-            )
-            copy.start()
-            later.append(copy)
-    for copy in later:
-        copy.wait_recv()
-    starts = [h * half + (firsts[h] * 4 + seconds[h]) * unit for h in range(2)]
-    for h in range(2):
-        mine = pl.ds(starts[h], unit)
-        plane[:, h] = terms[mine] + (got2[h, 0] + got2[h, 1]) + got2[h, 2]
-
-    def to_owner(step):
-        target = lax.rem(z + step, Z)
-        tile = jnp.minimum(target, OWNERS - 1)
-        return target, remote(
-            plane.at[tile], got3.at[step - 1], z_send.at[step], z_recv.at[step], device(x, y, target, core)
-        )
-
-    for step in order_of_z():
-        target, copy = to_owner(step)
-
-        @pl.when(target < OWNERS)
-        def _():
-            copy.start()
-
-    tile = jnp.minimum(z, OWNERS - 1)
-
-    def to_all(step):
-        return remote(
-            summed.at[tile], summed.at[tile], g_send.at[step], g_recv.at[step],
-            device(x, y, lax.rem(z + step, Z), core),
-        )
-
-    @pl.when(z < OWNERS)
-    def _():
-        for step in order_of_z():
-            to_owner(step)[1].wait_recv()
-        total = plane[tile]
-        for step in range(1, Z):
-            total = total + got3[step - 1]
-        summed[tile] = total
-        for step in order_of_z():
-            to_all(step).start()
-
-    for step in order_of_z():
-        source = lax.rem(z + Z - step, Z)
-
-        @pl.when(source < OWNERS)
-        def _():
-            to_all(step).wait_recv()
-
-    for h in range(2):
-        out[pl.ds(core * 2 * half + starts[h], unit)] = summed[:, h]
-    spread(out, unit, x, y, z, core, send, recv)
-
-    for step in range(1, Z):
-        target, copy = to_owner(step)
-
-        @pl.when(target < OWNERS)
-        def _():
-            copy.wait_send()
-
-    @pl.when(z < OWNERS)
-    def _():
-        for step in range(1, Z):
-            to_all(step).wait_send()
-
-    for copy in copies + later + pairs:
-        copy.wait_send()
+    add(theirs, True, 0, 2)
+    waves = [sum_wave(wave, out, terms, buffers[6 * wave:6 * wave + 6], sems[:-2], spot) for wave in range(2)]
+    next(waves[0])
+    add(theirs, True, 2, 4)
+    next(waves[1])
+    while waves:
+        waves = [wave for wave in waves if next(wave, waves) is None]
+    for pair in pairs:
+        pair.wait_send()
 
 
 def split(value):
@@ -635,25 +638,6 @@
             if start < stop:
                 up, down = split(mat[here, start:stop])
                 mat[here, start:stop] = dot(left, jnp.concatenate([up, up], axis=0)) + dot(high, down)
-        if after < NB:
-            turned_high, turned_low = split(mat[here, after:].T)
-            turned = jnp.concatenate([turned_high, turned_low], axis=1)
-
-            def change(begin, end, start, stop):
-                rows = slice(begin - after, end - after)
-                up, down = split(mat[here, start:stop])
-                return dot(turned[rows], jnp.concatenate([up, up], axis=0)) + dot(turned_high[rows], down)
-
-            following = slice(after, after + BLOCK)
-            corner = mat[following, following] - change(after, after + BLOCK, after, after + BLOCK)
-            own = jnp.concatenate(factor_block(lambda g: corner[8 * g:8 * g + 8, :], lane, row), axis=0)
-            mat[after:, here] = -change(after, NB, at, after)
-            for start in range(0, at, 256):
-                stop = min(start + 256, at)
-                mat[after:, start:stop] = mat[after:, start:stop] - change(after, NB, start, stop)
-            for start in range(after, NB, 256):
-                stop = min(start + 256, NB)
-                mat[after:stop, start:stop] = mat[after:stop, start:stop] - change(after, stop, start, stop)
         inverse = jnp.concatenate(
             [
                 mat[at + 64 * to_z + 16 * to_y + 8 * to_core:at + 64 * to_z + 16 * to_y + 8 * to_core + 8, :after]
@@ -672,31 +656,48 @@
         leave.start(0, k)
         if k:
             leave.start(1, k - 1)
+        if after < NB:
+            turned_high, turned_low = split(mat[here, after:].T)
+            turned = jnp.concatenate([turned_high, turned_low], axis=1)
+
+            def change(begin, end, start, stop):
+                rows = slice(begin - after, end - after)
+                up, down = split(mat[here, start:stop])
+                return dot(turned[rows], jnp.concatenate([up, up], axis=0)) + dot(turned_high[rows], down)
+
+            following = slice(after, after + BLOCK)
+            corner = mat[following, following] - change(after, after + BLOCK, after, after + BLOCK)
+            own = jnp.concatenate(factor_block(lambda g: corner[8 * g:8 * g + 8, :], lane, row), axis=0)
+            mat[after:, here] = -change(after, NB, at, after)
+            for start in range(0, at, 256):
+                stop = min(start + 256, at)
+                mat[after:, start:stop] = mat[after:, start:stop] - change(after, NB, start, stop)
+            for start in range(after, NB, 256):
+                stop = min(start + 256, NB)
+                mat[after:stop, start:stop] = mat[after:stop, start:stop] - change(after, stop, start, stop)
     leave.start(1, BLOCKS - 1)
 
 
 def whole_kernel(orbitals, piece, out, *scratch):
     buffers, sems = scratch[:BUFFERS], scratch[BUFFERS:]
     (
-        beside, landed, slab, rows, across, products, gram, theirs, terms, got0, got1, got2, got3,
-        plane, summed, mat, ready, beside2, landed2, ordered,
-    ) = buffers
+        beside, landed, slab, rows, across, products, gram, theirs, terms, mat, ready, beside2, landed2, ordered,
+    ) = buffers[:14]
     spot = place()
     greet(*spot, True)
     gather_part(orbitals, piece, slab, rows, across, beside, landed, sems[:7], sems[7:11], spot)
-    gram_part(across, slab, products, gram, theirs, terms, got0, got1, got2, got3, plane, summed, sems[11:21], spot)
+    gram_part(across, slab, products, gram, theirs, terms, buffers[14:], sems[11:21], spot)
     leave = Leave(ready, beside2, landed2, sems[21:26], spot)
     solve(gram, products, mat, leave)
     plane_part(landed2, ordered, out, leave.arrive, sems[26:29], spot)
     leave.finish()
 
 
-BUFFERS = 20
+BUFFERS = 26
 
 
 def whole(orbitals, piece):
     points = orbitals.shape[-1]
-    unit = OWNERS
     dma = pltpu.SemaphoreType.DMA
     narrow, wide = jnp.bfloat16, jnp.float32
     entries = (Z, Y, CORES, X, 2, points)
@@ -711,23 +712,26 @@
         pltpu.VMEM((TILES, 8, 128), wide),
         pltpu.VMEM((NB, points), narrow),
         pltpu.VMEM((TILES // 2, 8, 128), wide),
-        pltpu.VMEM((2, 2, 2 * unit, 8, 128), wide),
-        pltpu.VMEM((2, 2, 4 * unit, 8, 128), wide),
-        pltpu.VMEM((2, 3, unit, 8, 128), wide),
-        pltpu.VMEM((Z - 1, 2, 8, 128), wide),
-        pltpu.VMEM((OWNERS, 2, 8, 128), wide),
-        pltpu.VMEM((OWNERS, 2, 8, 128), wide),
         pltpu.VMEM((NB, NB), wide),
         pltpu.VMEM((BLOCKS, CORES, 2, held, points), narrow),
         pltpu.VMEM((BLOCKS, 2, held, points), narrow),
         pltpu.VMEM((Z, CORES, held, points), narrow),
         pltpu.VMEM((Z, CORES, Y, X, 2, points), narrow),
     ]
+    for unit in UNITS:
+        buffers += [
+            pltpu.VMEM((2, 2, 2 * unit, 8, 128), wide),
+            pltpu.VMEM((2, 2, 4 * unit, 8, 128), wide),
+            pltpu.VMEM((2, 3, unit, 8, 128), wide),
+            pltpu.VMEM((Z - 1, 2, 8, 128), wide),
+            pltpu.VMEM((unit, 2, 8, 128), wide),
+            pltpu.VMEM((unit, 2, 8, 128), wide),
+        ]
     sems = [
         dma, dma, dma((2, Z)), dma((2, Z)), dma((2, 4, X * Y)), dma((2, 4, X * Y)), dma((10,)),
         dma((Z,)), dma((Z,)), dma((3, 4)), dma((3, 4)),
-        dma((3, 2, 4)), dma((3, 2, 4)), dma((3, 2, 4)), dma((3, 2, 4)),
-        dma((Z,)), dma((Z,)), dma((Z,)), dma((Z,)), dma((4,)), dma((4,)),
+        dma((2, 3, 2, 4)), dma((2, 3, 2, 4)), dma((2, 3, 2, 4)), dma((2, 3, 2, 4)),
+        dma((2, Z)), dma((2, Z)), dma((2, Z)), dma((2, Z)), dma((4,)), dma((4,)),
         dma((BLOCKS,)), dma((BLOCKS,)), dma((2, Z)), dma((2, Z)), dma((2,)),
         dma((4, X * Y)), dma((4, X * Y)), dma((4,)),
     ]

time: 171 us -> 164 us (0.959)
  Pallas kernels: 167 us -> 160 us
    pallas_call x1, Pallas kernels: 167 us -> 160 us  [whole(): pl.pallas_call(whole_kernel, out_shape=jax.ShapeDtypeStruct(entries, narr...]
where the time goes in v5:
time: 164 us
  Pallas kernels  160 us (98%)
  local copies, waits for them, and re-layouts  2.14 us (1%)
    pallas_call x1, Pallas kernels, whole(): pl.pallas_call(whole_kernel, out_shape=jax.ShapeDtypeStruct(entries, narr...  160 us

profile of v5, /device:TPU:480, one launch (start us, length us, event | category | flops | bytes accessed | tf_op | source)
XLA Modules:
  0.0 164.0 jit_solution(6160395348643952260)
XLA Ops:
  0.0 0.7 add_select_fusion
  0.7 0.1 iota_compare_fusion.2
  0.8 1.1 copy.8
  1.9 0.2 copy.4
  2.1 0.0 copy-start
  2.1 1.2 select_reduce_fusion
  3.3 0.0 copy-done
  3.3 159.8 %localize.1 = bf16[16,4,2,4,2,256]{5,4,3,2,1,0:T(2,128)(2,1)S(1)} custom-call(bf16[16,4,2,4,2,256]{5,4,3,2,1,0:T(2,128)(2,1)S(1)} %bitcast.24, bf16[16,128]{1,0:T(8,128)(2,1)S(1)} %convert_element_type.13.piece), custom_call_target="tpu_custom_call" | custom-call | tf_op jit(solution)/shard_map/localize/pallas_call | solution.py:738
  163.2 0.8 copy.10
  (1 shorter events, 0.0 us)
Async XLA Ops:
  2.1 1.2 copy-start

commit v6 on v5

--- a/solution.py
+++ b/solution.py
@@ -142,11 +142,36 @@
             copy.wait_send()
 
 
-def gather_part(orbitals, piece, slab, rows, across, beside, landed, moving, sems, spot):
+def pick_part(orbitals, pivots, folded, chosen, piece):
+    points = orbitals.shape[-1]
+    for part in range(BLOCKS):
+        folded[part * BLOCK:(part + 1) * BLOCK, :] = orbitals[2 * part:2 * part + 2].reshape(BLOCK, points)
+    outer = pivots[...] // points
+    inner = pivots[...] - outer * points
+    lines = []
+    for orbital in range(2):
+        for part in range(BLOCKS):
+            index = lax.broadcasted_iota(jnp.int32, (BLOCK, NB), 0) + part * BLOCK
+            chosen[part * BLOCK:(part + 1) * BLOCK, :] = jnp.where(
+                index == 2 * outer + orbital, 1.0, 0.0
+            ).astype(jnp.bfloat16)
+        for start in range(0, NB, 256):
+            values = lax.dot_general(
+                folded[...], chosen[:, start:start + 256], (((0,), (0,)), ((), ())), preferred_element_type=jnp.float32
+            )
+            here = lax.broadcasted_iota(jnp.int32, values.shape, 0) == inner[:, start:start + 256]
+            line = jnp.sum(jnp.where(here, values, 0.0), axis=0, keepdims=True)
+            lines += [line[:, :128], line[:, 128:]]
+    piece[...] = jnp.concatenate(lines, axis=0).astype(jnp.bfloat16)
+
+
+def gather_part(orbitals, pivots, piece, slab, rows, across, folded, beside, landed, moving, sems, spot):
     q_send, q_recv, send, recv = sems
     x, y, z, core = spot
     regroup = Regroup(orbitals, slab, beside, landed, moving, (x, y, z, core))
     regroup.pair.start()
+    regroup.start_z(0)
+    pick_part(orbitals, pivots, folded, across, piece)
     first = []
     for step in order_of_z():
         copy = remote(
@@ -154,7 +179,6 @@
         )
         copy.start()
         first.append(copy)
-    regroup.start_z(0)
     regroup.start_z(1)
     rows[z, y, core, x] = piece[...]
     for copy in first:
@@ -678,25 +702,26 @@
     leave.start(1, BLOCKS - 1)
 
 
-def whole_kernel(orbitals, piece, out, *scratch):
+def whole_kernel(orbitals, pivots, out, *scratch):
     buffers, sems = scratch[:BUFFERS], scratch[BUFFERS:]
     (
         beside, landed, slab, rows, across, products, gram, theirs, terms, mat, ready, beside2, landed2, ordered,
-    ) = buffers[:14]
+        piece,
+    ) = buffers[:15]
     spot = place()
     greet(*spot, True)
-    gather_part(orbitals, piece, slab, rows, across, beside, landed, sems[:7], sems[7:11], spot)
-    gram_part(across, slab, products, gram, theirs, terms, buffers[14:], sems[11:21], spot)
+    gather_part(orbitals, pivots, piece, slab, rows, across, products, beside, landed, sems[:7], sems[7:11], spot)
+    gram_part(across, slab, products, gram, theirs, terms, buffers[15:], sems[11:21], spot)
     leave = Leave(ready, beside2, landed2, sems[21:26], spot)
     solve(gram, products, mat, leave)
     plane_part(landed2, ordered, out, leave.arrive, sems[26:29], spot)
     leave.finish()
 
 
-BUFFERS = 26
-
-
-def whole(orbitals, piece):
+BUFFERS = 27
+
+
+def whole(orbitals, pivots):
     points = orbitals.shape[-1]
     dma = pltpu.SemaphoreType.DMA
     narrow, wide = jnp.bfloat16, jnp.float32
@@ -717,6 +742,7 @@
         pltpu.VMEM((BLOCKS, 2, held, points), narrow),
         pltpu.VMEM((Z, CORES, held, points), narrow),
         pltpu.VMEM((Z, CORES, Y, X, 2, points), narrow),
+        pltpu.VMEM((16, 128), narrow),
     ]
     for unit in UNITS:
         buffers += [
@@ -743,23 +769,14 @@
         scratch_shapes=buffers + sems,
         compiler_params=pltpu.CompilerParams(collective_id=0, has_side_effects=True, vmem_limit_bytes=VMEM),
         name="localize",
-    )(orbitals, piece)
-
-
-def pick(orbitals, pivots):
-    folded = orbitals.reshape(2, 1024, 128)
-    outer = (pivots[:, None] // 128 == jnp.arange(1024, dtype=jnp.int32)[None, :]).astype(jnp.bfloat16)
-    inner = pivots[:, None] % 128 == jnp.arange(128, dtype=jnp.int32)[None, :]
-    rows = jnp.einsum("jh,rhl->rjl", outer, folded, preferred_element_type=jnp.float32)
-    return jnp.sum(jnp.where(inner[None], rows, 0.0), axis=2).astype(jnp.bfloat16)
+    )(orbitals, pivots)
 
 
 def body(orbitals, pivots):
     points = orbitals.shape[1] // 512
     entries = (Z, Y, CORES, X, 2, points)
-    piece = pick(orbitals, pivots).reshape(16, 128)
     outgoing = orbitals.reshape(2, 512, points).transpose(1, 0, 2).reshape(entries)
-    returned = whole(outgoing, piece)
+    returned = whole(outgoing, pivots.reshape(1, NB))
     return returned.reshape(512, 2, points).transpose(1, 0, 2).reshape(orbitals.shape)
 
 

time: 164 us -> 172 us (1.049)
  Pallas kernels: 160 us -> 169 us
    pallas_call x1, Pallas kernels: 160 us -> 169 us  [whole(): pl.pallas_call(whole_kernel, out_shape=jax.ShapeDtypeStruct(entries, narr...]
where the time goes in v6:
time: 172 us
  Pallas kernels  169 us (98%)
  local copies, waits for them, and re-layouts  2.52 us (1%)
    pallas_call x1, Pallas kernels, whole(): pl.pallas_call(whole_kernel, out_shape=jax.ShapeDtypeStruct(entries, narr...  169 us

profile of v6, /device:TPU:480, one launch (start us, length us, event | category | flops | bytes accessed | tf_op | source)
XLA Modules:
  0.0 171.5 jit_solution(2717742742288613339)
XLA Ops:
  0.0 0.0 copy-start
  0.0 1.0 copy-done
  1.0 0.0 copy-start.1
  1.0 0.7 copy-done.1
  1.7 169.0 %localize.1 = bf16[16,4,2,4,2,256]{5,4,3,2,1,0:T(2,128)(2,1)S(1)} custom-call(bf16[16,4,2,4,2,256]{5,4,3,2,1,0:T(2,128)(2,1)S(1)} %bitcast.12, s32[1,1024]{1,0:T(1,128)S(1)} %bitcast.13), custom_call_target="tpu_custom_call" | custom-call | tf_op jit(solution)/shard_map/localize/pallas_call | solution.py:764
  170.7 0.8 copy.6
Async XLA Ops:
  0.0 1.0 copy-start
  1.0 0.7 copy-start.1
